TPU v7x, 32 devices: a whole 2x2x4 slice. The times are simulated.
32 devices in a mesh: groups: 2 (over y), expert: 4 (over z), hidden: 4 (over x, core).
Axes of the slice: x: 2, y: 2, z: 4, core: 2. Of those that a mesh axis runs over, the one named last changes fastest.
Arguments:
- tokens: bfloat16 [1024, 6144], P(('groups', 'expert'), 'hidden'), parts along dimension 0, may hold values from -6 to 6
- cotangent: bfloat16 [1024, 6144], P(('groups', 'expert'), 'hidden'), parts along dimension 0, may hold values from -6 to 6
- routes: int32 [1024, 4], P(('groups', 'expert')), parts along dimension 0, may hold values from 0 to 15, as said below
- probs: bfloat16 [1024, 4], P(('groups', 'expert')), parts along dimension 0, may hold values from 0.049804688 to 1
- w_gate: bfloat16 [10752, 6144], P('expert', 'hidden'), may hold values from -0.078125 to 0.078125
- w_up: bfloat16 [10752, 6144], P('expert', 'hidden'), may hold values from -0.078125 to 0.078125
- w_down: bfloat16 [10752, 6144], P('expert', 'hidden'), may hold values from -0.0625 to 0.0625
Outputs:
- grad_tokens: bfloat16 [1024, 6144], P(('groups', 'expert'), 'hidden'), parts along dimension 0
- grad_probs: float32 [1024, 4], P(('groups', 'expert')), parts along dimension 0
- grad_gate: bfloat16 [21504, 6144], P(('groups', 'expert'), 'hidden'), parts along dimension 0
- grad_up: bfloat16 [21504, 6144], P(('groups', 'expert'), 'hidden'), parts along dimension 0
- grad_down: bfloat16 [21504, 6144], P(('groups', 'expert'), 'hidden'), parts along dimension 0
There are 2 independent parts, one for each index of `groups`. A program takes and returns all parts, laid end to end along the dimension named above; an argument that names none is the same for every part. Nothing has to cross between parts.
Inputs may be any that keep to these rules, and one draw needn't show every extreme that they name: `routes`: in every row the 4 ids are different. In each aligned block of 128 rows (the rows of one index of the expert axis) expert 0 is named by at most 8 rows, and by exactly 8 rows in at least one block.
All inputs are finite; a program needn't handle non-finite values.
Results may differ from a plain program's by a relative error of at most 0.0065.
Values may be sent and summed in bfloat16 or wider, within the bound.
No kernel may reach another device: no remote copies, remote signals or barrier semaphores. Data moves between devices by JAX's collectives and lax.ppermute only.
A program may use at most 128 MiB of HBM per device.

v0:
```python
import jax
import jax.numpy as jnp
from jax import lax
from jax.sharding import PartitionSpec as P

CAP = 8


def slot_table(routes, probs, capacity):
    chosen = routes == 0
    live = jnp.any(chosen, axis=1)
    weight = jnp.sum(jnp.where(chosen, probs, jnp.zeros_like(probs)), axis=1)
    order = jnp.cumsum(live.astype(jnp.int32)) - 1
    slots = lax.broadcasted_iota(jnp.int32, (capacity, routes.shape[0]), 0)
    hits = (order[None, :] == slots) & live[None, :]
    slot_weight = jnp.sum(jnp.where(hits, weight[None, :], jnp.zeros_like(weight)[None, :]), axis=1)
    return (chosen, hits, slot_weight)


def contract_last(left, right):
    return lax.dot_general(
        left, right, (((1,), (1,)), ((), ())), preferred_element_type=jnp.float32
    )


def contract_first(left, right):
    return lax.dot_general(
        left, right, (((0,), (0,)), ((), ())), preferred_element_type=jnp.float32
    )


def shards(tokens, cotangent, routes, probs, w_gate, w_up, w_down):
    chosen, hits, slot_weight = slot_table(routes, probs, CAP)
    picker = hits.astype(jnp.bfloat16)
    sent_x = jnp.dot(picker, tokens, preferred_element_type=jnp.float32).astype(jnp.bfloat16)
    sent_dy = jnp.dot(picker, cotangent, preferred_element_type=jnp.float32).astype(jnp.bfloat16)
    rows_x, rows_w = (
        lax.all_gather(sent_x, "expert", axis=0, tiled=True),
        lax.all_gather(slot_weight, "expert", axis=0, tiled=True),
    )
    gate_part = contract_last(rows_x, w_gate)
    up_part = contract_last(rows_x, w_up)
    gate, up = lax.psum((gate_part, up_part), "hidden")
    sig = jax.nn.sigmoid(gate)
    hidden_act = (gate * sig * up).astype(jnp.bfloat16)
    rows_dy = lax.all_gather(sent_dy, "expert", axis=0, tiled=True)
    back_part = contract_last(rows_dy, w_down)
    row_scale = rows_w.astype(jnp.float32)[:, None]
    back_hidden = lax.psum(back_part, "hidden")
    scaled = row_scale * back_hidden
    grad_gate_act = (scaled * up * sig * (1.0 + gate * (1.0 - sig))).astype(jnp.bfloat16)
    grad_up_act = (scaled * gate * sig).astype(jnp.bfloat16)
    dots = jnp.sum(hidden_act.astype(jnp.float32) * back_hidden, axis=1)
    weighted = (row_scale * rows_dy.astype(jnp.float32)).astype(jnp.bfloat16)
    grad_down = contract_first(hidden_act, weighted).astype(jnp.bfloat16)
    grad_gate = contract_first(grad_gate_act, rows_x).astype(jnp.bfloat16)
    grad_up = contract_first(grad_up_act, rows_x).astype(jnp.bfloat16)
    term = jnp.dot(grad_gate_act, w_gate, preferred_element_type=jnp.float32) + jnp.dot(
        grad_up_act, w_up, preferred_element_type=jnp.float32
    )
    returned, returned_dots = (
        lax.psum_scatter(term, "expert", scatter_dimension=0, tiled=True),
        lax.psum_scatter(dots, "expert", scatter_dimension=0, tiled=True),
    )
    spread = hits.astype(jnp.float32)
    grad_tokens = lax.dot_general(
        spread,
        returned,
        (((0,), (0,)), ((), ())),
        precision=lax.Precision.HIGHEST,
        preferred_element_type=jnp.float32,
    ).astype(jnp.bfloat16)
    token_dots = jnp.dot(returned_dots, spread, precision=lax.Precision.HIGHEST)
    grad_probs = jnp.where(chosen, token_dots[:, None], jnp.float32(0.0))
    return (grad_tokens, grad_probs, grad_gate, grad_up, grad_down)


def solution(mesh):
    placed = (
        P(("groups", "expert"), "hidden"),
        P(("groups", "expert"), "hidden"),
        P(("groups", "expert"), None),
        P(("groups", "expert"), None),
        P("expert", "hidden"),
        P("expert", "hidden"),
        P("expert", "hidden"),
    )
    return jax.shard_map(
        shards,
        mesh=mesh,
        in_specs=placed,
        out_specs=(
            P(("groups", "expert"), "hidden"),
            P(("groups", "expert"), None),
            P(("groups", "expert"), "hidden"),
            P(("groups", "expert"), "hidden"),
            P(("groups", "expert"), "hidden"),
        ),
        check_vma=False,
    )
```

profile of v0, /device:TPU:0, one launch (start us, length us, event | category | flops | bytes accessed | tf_op | source)
XLA Modules:
  0.0 135.3 jit_solution(10748588785824253544)
XLA Ops:
  7.2 0.0 all-reduce.5.cloned.1.call-start
  7.2 0.8 select_reduce_fusion
  8.0 0.1 copy.15
  8.1 0.2 reduce-window.8
  8.3 0.1 add_reduce_fusion
  8.4 0.2 convolution_convert_fusion.4
  8.6 15.2 %all_gather.11 = bf16[32,1536]{1,0:T(8,128)(2,1)S(1)} all-gather(bf16[8,1536]{1,0:T(8,128)(2,1)S(1)} %convolution_convert_fusion.4), channel_id=1, replica_groups=mesh['groups'=2,'expert'=4,'hidden'=4] {'expert'}, dimensions={0}, use_global_device_ids=true | all-gather | bytes 122880 | tf_op jit(solution)/shard_map/all_gather | solution.py:38
  23.8 6.7 %fusion.18 = f32[32,2688]{1,0:T(8,128)} fusion(bf16[32,1536]{1,0:T(8,128)(2,1)S(1)} %all_gather.11, bf16[2688,1536]{1,0:T(8,128)(2,1)} %param.12), kind=kOutput, calls=%fused_computation.35 | convolution fusion | flops 264241152 | bytes 8699904 | tf_op jit(solution)/shard_map/dot_general | solution.py:21
  30.4 3.2 %fusion.19 = f32[32,2688]{1,0:T(8,128)} fusion(bf16[32,1536]{1,0:T(8,128)(2,1)S(1)} %all_gather.11, bf16[2688,1536]{1,0:T(8,128)(2,1)S(1)} %copy-done.1), kind=kOutput, calls=%fused_computation.36 | convolution fusion | flops 264241152 | bytes 8699904 | tf_op jit(solution)/shard_map/dot_general | solution.py:21
  33.6 0.2 convolution_convert_fusion.5
  33.8 13.5 %all_gather.10 = bf16[32,1536]{1,0:T(8,128)(2,1)S(1)} all-gather(bf16[8,1536]{1,0:T(8,128)(2,1)S(1)} %convolution_convert_fusion.5), channel_id=1, replica_groups=mesh['groups'=2,'expert'=4,'hidden'=4] {'expert'}, dimensions={0}, use_global_device_ids=true | all-gather | bytes 122880 | tf_op jit(solution)/shard_map/all_gather | solution.py:46
  47.3 3.2 %fusion.17 = f32[32,2688]{1,0:T(8,128)} fusion(bf16[32,1536]{1,0:T(8,128)(2,1)S(1)} %all_gather.10, bf16[2688,1536]{1,0:T(8,128)(2,1)S(1)} %copy-done.2), kind=kOutput, calls=%fused_computation.34 | convolution fusion | flops 264241152 | bytes 8699904 | tf_op jit(solution)/shard_map/dot_general | solution.py:21
  50.5 0.0 all-reduce.5.cloned.1.call-update
  50.5 0.0 reduce-scatter.2.cloned.1.call-start
  50.5 0.6 fusion.16
  51.8 0.1 fusion.7
  51.9 0.2 dynamic-update-slice
  52.1 11.6 %all-reduce = bf16[32]{0:T(256)(128)(2,1)S(1)} all-reduce(bf16[32]{0:T(256)(128)(2,1)S(1)} %dynamic-update-slice), channel_id=1, replica_groups=mesh['groups'=2,'expert'=4,'hidden'=4] {'expert'}, use_global_device_ids=true, to_apply=%add | all-reduce | flops 32 | bytes 128
  64.4 23.3 %all-reduce.5.cloned.1.call-done = (f32[32,2688]{1,0:T(8,128)}, f32[32,2688]{1,0:T(8,128)}, f32[32,2688]{1,0:T(8,128)}) async-done(((f32[32,2688]{1,0:T(8,128)}, f32[32,2688]{1,0:T(8,128)}, f32[32,2688]{1,0:T(8,128)}), (f32[32,2688]{1,0:T(8,128)}, f32[32,2688]{1,0:T(8,128)}, f32[32,2688]{1,0:T(8,128)})) %all-reduce.5.cloned.1.call-update) | async-done | bytes 1032208 | tf_op jit(solution)/shard_map/psum | solution.py:43
  87.7 1.5 %multiply_reduce_fusion = (f32[32]{0:T(128)S(1)}, bf16[32,2688]{1,0:T(8,128)(2,1)S(1)}, bf16[32,2688]{1,0:T(8,128)(2,1)S(1)}, bf16[32,2688]{1,0:T(8,128)(2,1)S(1)}) fusion(f32[32,2688]{1,0:T(8,128)} %get-tuple-element.7, f32[32,2688]{1,0:T(8,128)} %get-tuple-element.6, f32[32,2688]{1,0:T(8,128)} %get-tuple-element.5, f32[32]{0:T(128)S(1)} %convert_element_type.62), kind=kLoop, calls=%fused_computation.8 | loop fusion | flops 1720288 | bytes 1548544 | tf_op jit(solution)/shard_map/reduce_sum | solution.py:53
  89.3 5.7 %convolution_convert_fusion = bf16[2688,1536]{1,0:T(8,128)(2,1)} fusion(bf16[32,2688]{1,0:T(8,128)(2,1)S(1)} %get-tuple-element.9, bf16[32,1536]{1,0:T(8,128)(2,1)S(1)} %all_gather.10, f32[32]{0:T(128)S(1)} %convert_element_type.62), kind=kOutput, calls=%fused_computation | convolution fusion | flops 268517376 | bytes 8528000 | tf_op jit(solution)/shard_map/dot_general | solution.py:27
  95.0 5.7 %convolution_convert_fusion.1 = bf16[2688,1536]{1,0:T(8,128)(2,1)} fusion(bf16[32,2688]{1,0:T(8,128)(2,1)S(1)} %get-tuple-element.13, bf16[32,1536]{1,0:T(8,128)(2,1)S(1)} %all_gather.11), kind=kOutput, calls=%fused_computation.1 | convolution fusion | flops 268369920 | bytes 8527872 | tf_op jit(solution)/shard_map/dot_general | solution.py:27
  100.7 1.5 %fusion.20 = f32[32,1536]{1,0:T(8,128)S(1)} fusion(bf16[32,2688]{1,0:T(8,128)(2,1)S(1)} %get-tuple-element.12, bf16[2688,1536]{1,0:T(8,128)(2,1)S(1)} %bitcast.28), kind=kOutput, calls=%fused_computation.37 | convolution fusion | flops 264241152 | bytes 8626176 | tf_op jit(solution)/shard_map/dot_general | solution.py:58
  102.2 0.7 slice-done.2
  102.8 1.2 slice-done.3
  104.1 2.2 %convolution_add_fusion = f32[32,1536]{1,0:T(8,128)} fusion(f32[32,1536]{1,0:T(8,128)S(1)} %fusion.20, bf16[32,2688]{1,0:T(8,128)(2,1)S(1)} %get-tuple-element.13, bf16[2688,1536]{1,0:T(8,128)(2,1)S(1)} %bitcast.30), kind=kOutput, calls=%fused_computation.4 | convolution fusion | flops 264290304 | bytes 8822784 | tf_op jit(solution)/shard_map/dot_general | solution.py:58
  106.3 11.9 %all-reduce.1 = f32[32]{0:T(128)S(1)} all-reduce(f32[32]{0:T(128)S(1)} %get-tuple-element.8), channel_id=3, replica_groups=mesh['groups'=2,'expert'=4,'hidden'=4] {'expert'}, use_global_device_ids=true, to_apply=%region_9.10.clone | all-reduce | flops 32 | bytes 256
  118.2 0.2 convolution_bitcast_fusion
  118.4 0.6 broadcast_select_fusion
  119.0 5.7 %convolution_convert_fusion.2 = bf16[2688,1536]{1,0:T(8,128)(2,1)} fusion(bf16[32,2688]{1,0:T(8,128)(2,1)S(1)} %get-tuple-element.12, bf16[32,1536]{1,0:T(8,128)(2,1)S(1)} %all_gather.11), kind=kOutput, calls=%fused_computation.2 | convolution fusion | flops 268369920 | bytes 8527872 | tf_op jit(solution)/shard_map/dot_general | solution.py:27
  124.7 1.7 %reduce-scatter.2.cloned.1.call-done = f32[8,1536]{1,0:T(8,128)} async-done(((f32[32,1536]{1,0:T(8,128)}), f32[8,1536]{1,0:T(8,128)}) %reduce-scatter.2.cloned.1.call-update) | async-done | bytes 49168 | tf_op jit(solution)/shard_map/reduce_scatter | solution.py:62
  126.4 2.1 %convolution_convert_fusion.3 = bf16[128,1536]{1,0:T(8,128)(2,1)} fusion(f32[8,1536]{1,0:T(8,128)} %reduce-scatter.2.cloned.1.call-done, s32[128]{0:T(128)S(1)} %add_reduce_fusion, pred[128]{0:T(512)(128)(4,1)S(1)} %reduce_or.9), kind=kOutput, calls=%fused_computation.3 | convolution fusion | flops 19073024 | bytes 443008 | tf_op jit(solution)/shard_map/dot_general | solution.py:66
  (23 shorter events, 0.1 us)
Async XLA Ops:
  7.2 1.2 copy-start
  7.2 80.5 %all-reduce.5.cloned.1.call-start = ((), (), s32[]{:S(2)}) async-start(), calls=%async_computation.2 | async-start | bytes 2064384 | tf_op jit(solution)/shard_map/psum | solution.py:43
  8.3 22.1 %copy-start.1 = (bf16[2688,1536]{1,0:T(8,128)(2,1)S(1)}, bf16[2688,1536]{1,0:T(8,128)(2,1)}, u32[]{:S(2)}) copy-start(bf16[2688,1536]{1,0:T(8,128)(2,1)} %param.11) | copy-start | bytes 24772612
  23.7 9.9 %copy-start.3 = (bf16[128,1536]{1,0:T(8,128)(2,1)S(1)}, bf16[128,1536]{1,0:T(8,128)(2,1)}, u32[]{:S(2)}) copy-start(bf16[128,1536]{1,0:T(8,128)(2,1)} %param.8) | copy-start | bytes 1179652
  23.7 23.5 %copy-start.2 = (bf16[2688,1536]{1,0:T(8,128)(2,1)S(1)}, bf16[2688,1536]{1,0:T(8,128)(2,1)}, u32[]{:S(2)}) copy-start(bf16[2688,1536]{1,0:T(8,128)(2,1)} %param.13) | copy-start | bytes 24772612
  30.4 20.1 %copy-start.4 = (u32[32]{0:T(128)S(1)}, u32[32]{0:T(128)}, u32[]{:S(2)}) copy-start(u32[32]{0:T(128)} %constant.21) | copy-start | bytes 388
  50.5 75.9 %reduce-scatter.2.cloned.1.call-start = ((), (), s32[]{:S(2)}) async-start(), calls=%async_computation.1 | async-start | bytes 245760 | tf_op jit(solution)/shard_map/reduce_scatter | solution.py:62
  89.3 11.4 %slice-start = ((s8[8257536]{0:T(1024)(128)(4,1)}), s8[4194304]{0:T(1024)(128)(4,1)S(1)}, s32[]{:S(2)}) async-start(s8[8257536]{0:T(1024)(128)(4,1)} %bitcast.27), calls=%async_computation.3 | async-start | bytes 8388608
  95.0 5.7 %slice-start.1 = ((s8[8257536]{0:T(1024)(128)(4,1)}), s8[4063232]{0:T(1024)(128)(4,1)S(1)}, s32[]{:S(2)}) async-start(s8[8257536]{0:T(1024)(128)(4,1)} %bitcast.27), calls=%async_computation.4 | async-start | bytes 8126464
  100.7 2.2 %slice-start.2 = ((s8[8257536]{0:T(1024)(128)(4,1)}), s8[4194304]{0:T(1024)(128)(4,1)S(1)}, s32[]{:S(2)}) async-start(s8[8257536]{0:T(1024)(128)(4,1)} %bitcast.29), calls=%async_computation.5 | async-start | bytes 8388608
  100.7 3.4 %slice-start.3 = ((s8[8257536]{0:T(1024)(128)(4,1)}), s8[4063232]{0:T(1024)(128)(4,1)S(1)}, s32[]{:S(2)}) async-start(s8[8257536]{0:T(1024)(128)(4,1)} %bitcast.29), calls=%async_computation.6 | async-start | bytes 8126464
Sparse Core Ops, SparseCore 0:
  50.6 37.0 all-reduce.4
  106.4 19.9 reduce-scatter.1
where the time goes:
time: 136 us; the launch traced here: 135 us
  blocking collectives  52.1 us (38%)
  matrix products  36.4 us (27%)
  waiting for transfers between devices  25 us (18%)
  between operations  15.4 us (11%)
  other arithmetic  3.32 us (2%)
  local copies, waits for them, and re-layouts  2.9 us (2%)
    unnamed x2, blocking collectives  23.5 us
    psum x1, waiting for transfers between devices, shards(): gate, up = lax.psum((gate_part, up_part), 'hidden')  23.3 us
    dot_general x3, matrix products, contract_first(): lax.dot_general(left, right, (((0,), (0,)), ((), ())), preferred_element_...  17.1 us
    all_gather x1, blocking collectives, shards(): lax.all_gather(sent_x, 'expert', axis=0, tiled=True)  15.2 us
    all_gather x1, blocking collectives, shards(): rows_dy = lax.all_gather(sent_dy, 'expert', axis=0, tiled=True)  13.5 us
    dot_general x3, matrix products, contract_last(): lax.dot_general(left, right, (((1,), (1,)), ((), ())), preferred_element_...  13.1 us
    unnamed x21, local copies, waits for them, and re-layouts  2.79 us
  transfers between devices with their start and end apart: 2, of which 2 were waited for; matrix products, arithmetic and copies ran while one was open for 5% of the time, Pallas kernels for 0%

commit v1 on v0

v1 whole, which is shorter than its diff:
```python
import functools

import jax
import jax.numpy as jnp
from jax import lax
from jax.experimental import pallas as pl
from jax.experimental.pallas import tpu as pltpu
from jax.sharding import PartitionSpec as P

CAP = 8
LANES = 128
F32 = jnp.float32
BF16 = jnp.bfloat16
SCALE = 32.0
WAIT_FLOPS = 3 * 10**10
FORWARD_ROWS, OUTER_ROWS, TERM_ROWS = 384, 384, 384
VMEM = pl.BlockSpec(memory_space=pltpu.VMEM)
HBM = pl.BlockSpec(memory_space=pltpu.HBM)


def slot_table(routes, probs, capacity):
    chosen = routes == 0
    live = jnp.any(chosen, axis=1)
    weight = jnp.sum(jnp.where(chosen, probs, jnp.zeros_like(probs)), axis=1)
    order = jnp.cumsum(live.astype(jnp.int32)) - 1
    slots = lax.broadcasted_iota(jnp.int32, (capacity, routes.shape[0]), 0)
    hits = (order[None, :] == slots) & live[None, :]
    slot_weight = jnp.sum(jnp.where(hits, weight[None, :], jnp.zeros_like(weight)[None, :]), axis=1)
    return (chosen, hits, slot_weight)


def contract(left, right, left_dim, right_dim):
    return lax.dot_general(
        left, right, (((left_dim,), (right_dim,)), ((), ())), preferred_element_type=F32
    )


def contract_last(left, right):
    return contract(left, right, 1, 1)


def contract_first(left, right):
    return contract(left, right, 0, 0)


def general_shards(tokens, cotangent, routes, probs, w_gate, w_up, w_down):
    chosen, hits, slot_weight = slot_table(routes, probs, CAP)
    picker = hits.astype(BF16)
    sent_x = jnp.dot(picker, tokens, preferred_element_type=F32).astype(BF16)
    sent_dy = jnp.dot(picker, cotangent, preferred_element_type=F32).astype(BF16)
    rows_x, rows_w = (
        lax.all_gather(sent_x, "expert", axis=0, tiled=True),
        lax.all_gather(slot_weight, "expert", axis=0, tiled=True),
    )
    gate_part = contract_last(rows_x, w_gate)
    up_part = contract_last(rows_x, w_up)
    gate, up = lax.psum((gate_part, up_part), "hidden")
    sig = jax.nn.sigmoid(gate)
    hidden_act = (gate * sig * up).astype(BF16)
    rows_dy = lax.all_gather(sent_dy, "expert", axis=0, tiled=True)
    back_part = contract_last(rows_dy, w_down)
    row_scale = rows_w.astype(F32)[:, None]
    back_hidden = lax.psum(back_part, "hidden")
    scaled = row_scale * back_hidden
    grad_gate_act = (scaled * up * sig * (1.0 + gate * (1.0 - sig))).astype(BF16)
    grad_up_act = (scaled * gate * sig).astype(BF16)
    dots = jnp.sum(hidden_act.astype(F32) * back_hidden, axis=1)
    weighted = (row_scale * rows_dy.astype(F32)).astype(BF16)
    grad_down = contract_first(hidden_act, weighted).astype(BF16)
    grad_gate = contract_first(grad_gate_act, rows_x).astype(BF16)
    grad_up = contract_first(grad_up_act, rows_x).astype(BF16)
    term = jnp.dot(grad_gate_act, w_gate, preferred_element_type=F32) + jnp.dot(
        grad_up_act, w_up, preferred_element_type=F32
    )
    returned, returned_dots = (
        lax.psum_scatter(term, "expert", scatter_dimension=0, tiled=True),
        lax.psum_scatter(dots, "expert", scatter_dimension=0, tiled=True),
    )
    spread = hits.astype(F32)
    grad_tokens = lax.dot_general(
        spread,
        returned,
        (((0,), (0,)), ((), ())),
        precision=lax.Precision.HIGHEST,
        preferred_element_type=F32,
    ).astype(BF16)
    token_dots = jnp.dot(returned_dots, spread, precision=lax.Precision.HIGHEST)
    grad_probs = jnp.where(chosen, token_dots[:, None], F32(0.0))
    return (grad_tokens, grad_probs, grad_gate, grad_up, grad_down)


def slots_of(routes, up_to):
    count = routes.shape[1]
    chosen = routes == 0
    live = jnp.max(jnp.where(chosen, F32(1.0), F32(0.0)), axis=0, keepdims=True)
    live_rows = jnp.broadcast_to(live, (CAP, count))
    order = contract(live_rows.astype(BF16), up_to, 1, 0)
    slots = lax.broadcasted_iota(jnp.int32, (CAP, count), 0).astype(F32) + 1.0
    hits = jnp.where(order == slots, live_rows, F32(0.0))
    return chosen, hits


def triangle_kernel(up_to):
    dims = up_to.shape
    here = lax.broadcasted_iota(jnp.int32, dims, 0) <= lax.broadcasted_iota(jnp.int32, dims, 1)
    up_to[...] = jnp.where(here, F32(1.0), F32(0.0)).astype(BF16)


def pick_kernel(up_to, routes, probs, tokens, cotangent, sent):
    chosen, hits = slots_of(routes[...], up_to[...])
    weight = jnp.sum(jnp.where(chosen, probs[...].astype(F32), F32(0.0)), axis=0, keepdims=True)
    picker = hits.astype(BF16)
    width = tokens.shape[1]
    sent[:, :width] = contract(picker, tokens[...], 1, 0).astype(BF16)
    sent[:, width : 2 * width] = contract(picker, cotangent[...], 1, 0).astype(BF16)
    slot_weight = jnp.sum(hits * weight, axis=1, keepdims=True)
    sent[:, 2 * width :] = jnp.broadcast_to(slot_weight, (CAP, LANES)).astype(BF16)


def ordered(blocks, core):
    half = len(blocks) // 2
    wide = [block.astype(F32) for block in blocks]
    turned = wide[half:] + wide[:half]
    return jnp.concatenate(
        [jnp.where(core == 0, a, b) for a, b in zip(wide, turned)], axis=0
    )


def pieces(size, wanted):
    return [slice(at, min(at + wanted, size)) for at in range(0, size, wanted)]


def forward_spans(spans, x, dy, weights, sums):
    half = x.shape[0] // 2
    for at, span in enumerate(spans):
        mine, theirs = sums[2 * at], sums[2 * at + 1]
        for part in pieces(span.stop - span.start, FORWARD_ROWS):
            rows = slice(span.start + part.start, span.start + part.stop)
            for which, (left, right) in enumerate(zip(weights, (x, x, dy))):
                value = contract(left[rows, :], right, 1, 1).T
                mine[which * half : (which + 1) * half, part] = value[:half]
                theirs[which * half : (which + 1) * half, part] = value[half:]


def forward_first_kernel(
    spans, b3, b2, b1, b0, w_gate, w_up, w_down, rows_x, rows_dy, weighted, scale, *sums
):
    core = lax.rem(lax.axis_index("hidden"), 2)
    width = w_gate.shape[1]
    blocks = ordered([b0[...], b1[...], b2[...], b3[...]], core)
    x = blocks[:, :width].astype(BF16)
    dy32 = blocks[:, width : 2 * width]
    dy = dy32.astype(BF16)
    row_scale = blocks[:, 2 * width :]
    rows_x[...] = x
    rows_dy[...] = dy
    weighted[...] = (row_scale[:, :1] * dy32).astype(BF16)
    scale[...] = row_scale
    forward_spans(spans, x, dy, (w_gate, w_up, w_down), sums)


def forward_next_kernel(spans, x, dy, w_gate, w_up, w_down, *rest):
    sums = rest[-2 * len(spans) :]
    forward_spans(spans, x[...], dy[...], (w_gate, w_up, w_down), sums)


def rounded(value):
    spread = value * 8193.0
    short = spread - (spread - value)
    return jnp.where(jnp.abs(short) < 2.0**-14, F32(0.0), short)


def add_kernel(*refs):
    total = refs[-1]
    at = 0
    for mine, got in zip(refs[:-1:2], refs[1:-1:2]):
        size = mine.shape[1]
        total[:, at : at + size] = rounded((mine[...] + got[...]) * SCALE)
        at += size


def activations(own, other, scale, acts):
    half = own.shape[0] // 3
    row_scale = scale[:half, :1]
    dots = jnp.zeros((half, 1), F32)
    for part in pieces(own.shape[1], 384):
        total = (own[:, part] + other[:, part]) * (1.0 / SCALE)
        gate, up, back = total[:half], total[half : 2 * half], total[2 * half :]
        sig = jax.nn.sigmoid(gate)
        hidden_act = (gate * sig * up).astype(BF16)
        scaled = row_scale * back
        acts[:half, part] = hidden_act
        acts[half : 2 * half, part] = (scaled * up * sig * (1.0 + gate * (1.0 - sig))).astype(BF16)
        acts[2 * half :, part] = (scaled * gate * sig).astype(BF16)
        dots = dots + jnp.sum(hidden_act.astype(F32) * back, axis=1, keepdims=True)
    return dots


def act_first_kernel(own, other, scale, after, acts, dots):
    dots[...] = jnp.broadcast_to(activations(own, other, scale, acts), dots.shape)


def act_last_kernel(own, other, scale, dots_before, after, acts):
    half, width = own.shape[0] // 3, own.shape[1]
    dots = dots_before[:, :1] + activations(own, other, scale, acts)
    high = dots.astype(BF16)
    rest = dots - high.astype(F32)
    middle = rest.astype(BF16)
    low = (rest - middle.astype(F32)).astype(BF16)
    for at, value in enumerate((high, middle, low)):
        acts[at * half : (at + 1) * half, width:] = jnp.broadcast_to(value, (half, LANES))


def both_rows(mine, theirs, at, part):
    half = mine.shape[0] // 3
    here = slice(at * half, (at + 1) * half)
    return jnp.concatenate([mine[here, part], theirs[here, part]], axis=0)


def outer_copies(jobs, staged, sems):
    found = []
    base = 0
    for acts, at, right, out, offset, size in jobs:
        for part in pieces(size, OUTER_ROWS):
            put = slice(base + part.start, base + part.stop)
            target = out.at[slice(offset + part.start, offset + part.stop), :]
            copy = pltpu.make_async_copy(staged.at[put, :], target, sems.at[len(found)])
            found.append((acts, at, right, part, put, copy))
        base += size
    return found


def outer_pieces(jobs, staged, sems):
    found = outer_copies(jobs, staged, sems)
    for acts, at, right, part, put, copy in found:
        staged[put, :] = contract_first(both_rows(*acts, at, part), right[...]).astype(BF16)
        copy.start()
    return [copy for *_, copy in found]


def token_terms(acts, w_gate, w_up, offset, size):
    total = None
    for part in pieces(size, TERM_ROWS):
        rows = slice(offset + part.start, offset + part.stop)
        value = contract(both_rows(*acts, 1, part), w_gate[rows, :], 1, 0)
        value = value + contract(both_rows(*acts, 2, part), w_up[rows, :], 1, 0)
        total = value if total is None else total + value
    return total


def gradients_first_kernel(
    cut, mine, theirs, rows_x, weighted, w_gate, w_up, term, grad_down, grad_gate, staged, sems
):
    core = lax.rem(lax.axis_index("hidden"), 2)
    acts = (mine, theirs)
    jobs = [(acts, 0, weighted, grad_down, 0, cut), (acts, 1, rows_x, grad_gate, 0, cut)]
    copies = outer_pieces(jobs, staged, sems)

    @pl.when(core < 2)
    def products():
        term[...] = token_terms(acts, w_gate, w_up, 0, cut)

    for copy in copies:
        copy.wait()


def up_kernel(size, mine, theirs, rows_x, after, up_here):
    for part in pieces(size, OUTER_ROWS):
        up_here[part, :] = contract_first(both_rows(mine, theirs, 2, part), rows_x[...]).astype(BF16)


def gradients_last_kernel(
    cut, mine, theirs, w_gate, w_up, term, up_here, o0, o1, o2, o3, grad_up, up_sem
):
    core = lax.rem(lax.axis_index("hidden"), 2)
    half = mine.shape[0] // 3
    hidden, width = w_gate.shape
    up_copy = pltpu.make_async_copy(up_here, grad_up.at[slice(0, cut), :], up_sem)
    up_copy.start()

    @pl.when(core < 2)
    def products():
        total = term[...] + token_terms((mine, theirs), w_gate, w_up, cut, hidden - cut)

        def dots_of(ref):
            tail = ref[:, hidden - cut :].astype(F32)
            return tail[:half] + tail[half : 2 * half] + tail[2 * half :]

        dots = jnp.concatenate([dots_of(mine), dots_of(theirs)], axis=0)
        outs = (o0, o1, o2, o3)
        for at, out in enumerate(outs):
            here = slice(at * CAP, (at + 1) * CAP)
            turn = (at + len(outs) // 2) % len(outs)
            there = slice(turn * CAP, (turn + 1) * CAP)
            out[:, :width] = jnp.where(core == 0, total[here], total[there])
            out[:, width:] = jnp.where(core == 0, dots[here], dots[there])

    up_copy.wait()


def gradients_rest_kernel(
    cut, mine, theirs, rows_x, weighted, down_before, gate_before,
    up_here, grad_down, grad_gate, staged, sems,
):
    core = lax.rem(lax.axis_index("hidden"), 2)
    acts, rest = (mine, theirs), grad_gate.shape[0] - cut
    jobs = [(acts, 0, weighted, grad_down, cut, rest), (acts, 1, rows_x, grad_gate, cut, rest)]
    copies = outer_pieces(jobs, staged, sems)

    @pl.when(core < 2)
    def up():
        up_kernel(rest, mine, theirs, rows_x, None, up_here)

    for copy in copies:
        copy.wait()


def place_kernel(
    cut, up_to, routes, r3, r2, r1, r0, up_here, up_before,
    grad_tokens, grad_probs, grad_up, placed, placed_probs, sems,
):
    core = lax.rem(lax.axis_index("hidden"), 2)
    rest = grad_up.shape[0] - cut
    up_copy = pltpu.make_async_copy(up_here, grad_up.at[slice(cut, cut + rest), :], sems.at[0])
    up_copy.start()
    copies = [
        pltpu.make_async_copy(placed, grad_tokens, sems.at[1]),
        pltpu.make_async_copy(placed_probs, grad_probs, sems.at[2]),
    ]

    @pl.when(core < 2)
    def place():
        chosen, hits = slots_of(routes[...], up_to[...])
        total = r0[...] + r1[...] + r2[...] + r3[...]
        width = grad_tokens.shape[1]
        placed[...] = contract_first(hits.astype(BF16), total[:, :width].astype(BF16)).astype(BF16)
        token_dots = jnp.sum(hits * total[:, width : width + 1], axis=0, keepdims=True)
        placed_probs[...] = jnp.where(chosen, token_dots, F32(0.0))

    for copy in copies:
        copy.start()
    up_copy.wait()
    for copy in copies:
        copy.wait()


def shape(dims, dtype):
    return jax.ShapeDtypeStruct(dims, dtype)


def params(mebibytes):
    return pltpu.CompilerParams(vmem_limit_bytes=mebibytes << 20)


def paired_shards(tokens, cotangent, routes, probs, w_gate, w_up, w_down):
    tokens_here, width = tokens.shape
    hidden = w_gate.shape[0]
    rows = 4 * CAP
    half = rows // 2
    routes_t, probs_t = routes.T, probs.T

    def swap(value, axis, bit):
        return lax.ppermute(value, axis, [(i, i ^ bit) for i in range(4)])

    up_to = pl.pallas_call(
        triangle_kernel,
        in_specs=[],
        out_specs=VMEM,
        out_shape=shape((tokens_here, tokens_here), BF16),
        compiler_params=params(1),
        cost_estimate=pl.CostEstimate(flops=WAIT_FLOPS, bytes_accessed=0, transcendentals=0),
        name="triangle",
    )()
    sent = pl.pallas_call(
        pick_kernel,
        in_specs=[VMEM] * 5,
        out_specs=VMEM,
        out_shape=shape((CAP, 2 * width + LANES), BF16),
        compiler_params=params(2),
        name="pick_rows",
    )(up_to, routes_t, probs_t, tokens, cotangent)
    got = [swap(sent, "expert", bit) for bit in (3, 2, 1)]

    def exchange(own):
        return own, swap(own.astype(jnp.float16), "hidden", 2)

    weights = (w_gate, w_up, w_down)
    tiles = hidden // LANES
    cuts = [LANES * at for at in (0, tiles // 2, tiles // 2 + 4, tiles // 2 + 7, tiles)]
    spans = [slice(a, b) for a, b in zip(cuts, cuts[1:])]
    cut = cuts[1]
    rest = hidden - cut

    def cost(products, size):
        return pl.CostEstimate(
            flops=16 * products * rows * size * width, bytes_accessed=0, transcendentals=0
        )

    def call(kernel, name, outs, args, limit=4, **more):
        single = not isinstance(outs, list)
        return pl.pallas_call(
            kernel,
            in_specs=[VMEM] * len(args),
            out_specs=VMEM if single else [VMEM] * len(outs),
            out_shape=outs,
            compiler_params=params(limit),
            name=name,
            **more,
        )(*args)

    def sums(some):
        return [shape((3 * half, span.stop - span.start), F32) for span in some for _ in range(2)]

    rows_x, rows_dy, weighted, scale, mine_a, theirs_a = call(
        functools.partial(forward_first_kernel, spans[:1]),
        "forward_first",
        [shape((rows, width), BF16)] * 3 + [shape((rows, LANES), F32)] + sums(spans[:1]),
        (*got, sent, *weights),
        limit=8,
        cost_estimate=cost(3, cut),
    )
    core_a = swap(theirs_a, "hidden", 1)

    def forward_next(some, after):
        found = call(
            functools.partial(forward_next_kernel, some),
            "forward_next",
            sums(some),
            (rows_x, rows_dy, *weights, *after),
            cost_estimate=cost(3, some[-1].stop - some[0].start),
        )
        return [(m, swap(t, "hidden", 1)) for m, t in zip(found[::2], found[1::2])]

    pairs = forward_next(spans[1:2], ())
    total_a = call(add_kernel, "core_sum_first", shape((3 * half, cut), F32), (mine_a, core_a))
    own_a, other_a = exchange(total_a)
    pairs += forward_next(spans[2:], (own_a,))
    total_b = call(
        add_kernel, "core_sum_last", shape((3 * half, rest), F32), [ref for pair in pairs for ref in pair]
    )
    own_b, other_b = exchange(total_b)

    acts_a, dots_a = call(
        act_first_kernel,
        "activations_first",
        [shape((3 * half, cut), BF16), shape((half, LANES), F32)],
        (own_a, other_a.astype(F32), scale, total_b),
    )
    first = (acts_a, swap(acts_a, "hidden", 1))
    whole = shape((hidden, width), BF16)
    term, down_a, gate_a = pl.pallas_call(
        functools.partial(gradients_first_kernel, cut),
        in_specs=[VMEM] * 6,
        out_specs=[VMEM, HBM, HBM],
        out_shape=[shape((rows, width), F32), whole, whole],
        scratch_shapes=[
            pltpu.VMEM((2 * cut, width), BF16),
            pltpu.SemaphoreType.DMA((2 * len(pieces(cut, OUTER_ROWS)),)),
        ],
        compiler_params=params(12),
        name="gradients_first",
    )(*first, rows_x, weighted, w_gate, w_up)
    other_b, term = lax.optimization_barrier((other_b, term))
    acts_b = call(
        act_last_kernel,
        "activations_last",
        shape((3 * half, rest + LANES), BF16),
        (own_b, other_b.astype(F32), scale, dots_a, term),
    )
    last = (acts_b, swap(acts_b, "hidden", 1))
    up_first = call(
        functools.partial(up_kernel, cut),
        "up_gradient_first",
        shape((cut, width), BF16),
        (*first, rows_x, acts_b),
    )
    *parts, up_a = pl.pallas_call(
        functools.partial(gradients_last_kernel, cut),
        in_specs=[VMEM] * 6,
        out_specs=[VMEM] * 4 + [HBM],
        out_shape=[shape((CAP, width + LANES), F32)] * 4 + [whole],
        scratch_shapes=[pltpu.SemaphoreType.DMA],
        compiler_params=params(4),
        name="gradients_last",
    )(*last, w_gate, w_up, term, up_first)
    back = [swap(parts[bit], "expert", bit) for bit in (3, 2, 1)]

    up_last, grad_down, grad_gate = pl.pallas_call(
        functools.partial(gradients_rest_kernel, cut),
        in_specs=[VMEM] * 4 + [HBM] * 2,
        out_specs=[VMEM, HBM, HBM],
        out_shape=[shape((rest, width), BF16), whole, whole],
        scratch_shapes=[
            pltpu.VMEM((2 * rest, width), BF16),
            pltpu.SemaphoreType.DMA((2 * len(pieces(rest, OUTER_ROWS)),)),
        ],
        input_output_aliases={4: 1, 5: 2},
        compiler_params=params(12),
        cost_estimate=cost(3, rest),
        name="gradients_rest",
    )(*last, rows_x, weighted, down_a, gate_a)

    grad_tokens, grad_probs, grad_up = pl.pallas_call(
        functools.partial(place_kernel, cut),
        in_specs=[VMEM] * 7 + [HBM],
        out_specs=[HBM] * 3,
        out_shape=[shape((tokens_here, width), BF16), shape(routes_t.shape, F32), whole],
        scratch_shapes=[
            pltpu.VMEM((tokens_here, width), BF16),
            pltpu.VMEM(routes_t.shape, F32),
            pltpu.SemaphoreType.DMA((3,)),
        ],
        input_output_aliases={7: 2},
        compiler_params=params(4),
        name="place_rows",
    )(up_to, routes_t, *back, parts[0], up_last, up_a)
    return (grad_tokens, grad_probs.T, grad_gate, grad_up, grad_down)


def solution(mesh):
    placed = (
        P(("groups", "expert"), "hidden"),
        P(("groups", "expert"), "hidden"),
        P(("groups", "expert"), None),
        P(("groups", "expert"), None),
        P("expert", "hidden"),
        P("expert", "hidden"),
        P("expert", "hidden"),
    )

    def shards(tokens, cotangent, routes, probs, w_gate, w_up, w_down):
        paired = mesh.shape["expert"] == 4 and mesh.shape["hidden"] == 4
        paired = paired and w_gate.shape[0] % LANES == 0 and w_gate.shape[1] % LANES == 0
        plan = paired_shards if paired else general_shards
        return plan(tokens, cotangent, routes, probs, w_gate, w_up, w_down)

    return jax.shard_map(
        shards,
        mesh=mesh,
        in_specs=placed,
        out_specs=(
            P(("groups", "expert"), "hidden"),
            P(("groups", "expert"), None),
            P(("groups", "expert"), "hidden"),
            P(("groups", "expert"), "hidden"),
            P(("groups", "expert"), "hidden"),
        ),
        check_vma=False,
    )
```

time: 136 us -> 43.4 us (0.32)
  blocking collectives: 52.1 us -> 0 us
  matrix products: 36.4 us -> 0 us
  Pallas kernels: 0 us -> 20.8 us
  waiting for transfers between devices: 25 us -> 6.63 us
  between operations: 15.4 us -> 0.83 us
  starting transfers between devices: 0.08 us -> 13.8 us
  other arithmetic: 3.32 us -> 0.07 us
  local copies, waits for them, and re-layouts: 2.9 us -> 1.08 us
    dot_general x12 -> x0, matrix products: 36.4 us -> none  [the longest x3 17.1 us: contract_first(): lax.dot_general(left, right, (((0,), (0,)), ((), ())), preferred_element_...]
    all_gather x2 -> x0, blocking collectives: 28.6 us -> none  [the longest x1 15.2 us: shards(): lax.all_gather(sent_x, 'expert', axis=0, tiled=True)]
    unnamed x2 -> x0, blocking collectives: 23.5 us -> none
    psum x1 -> x0, waiting for transfers between devices: 23.3 us -> none  [shards(): gate, up = lax.psum((gate_part, up_part), 'hidden')]
    pallas_call x0 -> x14, Pallas kernels: none -> 20.8 us  [the longest x8 8.71 us: call(): pl.pallas_call(kernel, in_specs=[VMEM] * len(args), out_specs=VMEM if sin...]
    ppermute x0 -> x14, starting transfers between devices: none -> 13.8 us  [swap(): return lax.ppermute(value, axis, [(i, i ^ bit) for i in range(4)])]
    ppermute x0 -> x14, waiting for transfers between devices: none -> 6.63 us  [swap(): return lax.ppermute(value, axis, [(i, i ^ bit) for i in range(4)])]
    reduce_sum x3 -> x0, other arithmetic: 2.41 us -> none  [the longest x1 1.54 us: shards(): dots = jnp.sum(hidden_act.astype(jnp.float32) * back_hidden, axis=1)]
  transfers between devices with their start and end apart: 2 -> 14, of which waited for: 2 -> 4; matrix products, arithmetic and copies ran while one was open for 5% -> 0% of each run, Pallas kernels for 0% -> 30%
where the time goes in v1:
time: 43.4 us; the launch traced here: 43.2 us
  Pallas kernels  20.8 us (48%)
  starting transfers between devices  13.8 us (32%)
  waiting for transfers between devices  6.63 us (15%)
  local copies, waits for them, and re-layouts  1.08 us (2%)
  between operations  0.83 us (2%)
    ppermute x14, starting transfers between devices, swap(): return lax.ppermute(value, axis, [(i, i ^ bit) for i in range(4)])  13.8 us
    pallas_call x8, Pallas kernels, call(): pl.pallas_call(kernel, in_specs=[VMEM] * len(args), out_specs=VMEM if sin...  8.71 us
    ppermute x14, waiting for transfers between devices, swap(): return lax.ppermute(value, axis, [(i, i ^ bit) for i in range(4)])  6.63 us
    pallas_call x1, Pallas kernels, paired_shards(): pl.pallas_call(functools.partial(gradients_rest_kernel, cut), in_specs=[V...  3.92 us
    pallas_call x1, Pallas kernels, paired_shards(): pl.pallas_call(functools.partial(gradients_first_kernel, cut), in_specs=[...  3.7 us
    pallas_call x1, Pallas kernels, paired_shards(): pl.pallas_call(functools.partial(place_kernel, cut), in_specs=[VMEM] * 7...  2.2 us
    pallas_call x1, Pallas kernels, paired_shards(): pl.pallas_call(functools.partial(gradients_last_kernel, cut), in_specs=[V...  1.93 us
    unnamed x14, local copies, waits for them, and re-layouts  1.08 us
  transfers between devices with their start and end apart: 14, of which 4 were waited for; matrix products, arithmetic and copies ran while one was open for 0% of the time, Pallas kernels for 30%

profile of v1, /device:TPU:0, one launch (start us, length us, event | category | flops | bytes accessed | tf_op | source)
XLA Modules:
  0.0 43.2 jit_solution(1665583728594005453)
XLA Ops:
  0.7 0.6 %copy-done.5 = s32[128,4]{0,1:T(4,128)S(1)} copy-done((s32[128,4]{0,1:T(4,128)S(1)}, s32[128,4]{0,1:T(4,128)}, u32[]{:S(2)}) %copy-start.5) | copy-done | bytes 2072
  1.3 0.3 copy-done.3
  1.7 0.1 copy-done.4
  1.8 0.3 pick_rows.1.b0
  2.1 5.1 %collective-permute-start = (bf16[8,3200]{1,0:T(8,128)(2,1)S(1)}, bf16[8,3200]{1,0:T(8,128)(2,1)S(1)}, u32[]{:S(2)}, u32[]{:S(2)}) collective-permute-start(bf16[8,3200]{1,0:T(8,128)(2,1)S(1)} %pick_rows.1.b0), channel_id=1, source_target_pairs={{0,12},{4,8},{8,4},{12,0},{1,13},{5,9},{9,5},{13,1},{2,14},{6,10},... | collective-permute-start | bytes 153608 | tf_op jit(solution)/shard_map/ppermute | solution.py:363
  7.2 0.6 %collective-permute-start.2 = (bf16[8,3200]{1,0:T(8,128)(2,1)S(1)}, bf16[8,3200]{1,0:T(8,128)(2,1)S(1)}, u32[]{:S(2)}, u32[]{:S(2)}) collective-permute-start(bf16[8,3200]{1,0:T(8,128)(2,1)S(1)} %pick_rows.1.b0), channel_id=1, source_target_pairs={{0,4},{4,0},{8,12},{12,8},{1,5},{5,1},{9,13},{13,9},{2,6},{6,2},{1... | collective-permute-start | bytes 153608 | tf_op jit(solution)/shard_map/ppermute | solution.py:363
  7.8 1.6 %collective-permute-done.b3 = bf16[8,3200]{1,0:T(8,128)(2,1)S(1)} collective-permute-done((bf16[8,3200]{1,0:T(8,128)(2,1)S(1)}, bf16[8,3200]{1,0:T(8,128)(2,1)S(1)}, u32[]{:S(2)}, u32[]{:S(2)}) %collective-permute-start) | collective-permute-done | bytes 51232 | tf_op jit(solution)/shard_map/ppermute | solution.py:363
  9.5 2.7 %collective-permute-done.1.b2 = bf16[8,3200]{1,0:T(8,128)(2,1)S(1)} collective-permute-done((bf16[8,3200]{1,0:T(8,128)(2,1)S(1)}, bf16[8,3200]{1,0:T(8,128)(2,1)S(1)}, u32[]{:S(2)}, u32[]{:S(2)}) %collective-permute-start.1) | collective-permute-done | bytes 51232 | tf_op jit(solution)/shard_map/ppermute | solution.py:363
  12.2 3.3 %forward_first.1 = (bf16[32,1536]{1,0:T(8,128)(2,1)S(1)}, bf16[32,1536]{1,0:T(8,128)(2,1)S(1)}, bf16[32,1536]{1,0:T(8,128)(2,1)S(1)}, f32[32,128]{1,0:T(8,128)S(...) custom-call(bf16[8,3200]{1,0:T(8,128)(2,1)S(1)} %collective-permute-done.b3, ...), custom_call_target="tpu_custom_call" | custom-call | flops 3019898880 | tf_op jit(solution)/shard_map/forward_first/pallas_call | solution.py:401
  15.5 0.1 collective-permute-start.4
  15.5 1.4 %forward_next.2 = (f32[48,512]{1,0:T(8,128)S(1)}, f32[48,512]{1,0:T(8,128)S(1)}) custom-call(bf16[32,1536]{1,0:T(8,128)(2,1)S(1)} %get-tuple-element.35.x.rows_x, bf16[32,1536]{1,0:T(8,128)(2,1)S(1)} %get-tuple-element.36.dy, bf16[2688,1536]{1,0:T(8,128)(2,1)S(1)} %copy-done, bf16[2688,1536]{1,0:T(8,128)(2,1)S(1)} %copy-done.1, bf16[2688,1536]{1,0:T(8,128)(2,1)S(1)} %copy-done.2), custom_call_target="tpu_custom_call" | custom-call | flops 1207959552 | tf_op jit(solution)/shard_map/forward_next/pallas_call | solution.py:401
  17.0 0.5 %collective-permute-start.3 = (f32[48,512]{1,0:T(8,128)S(1)}, f32[48,512]{1,0:T(8,128)S(1)}, u32[]{:S(2)}, u32[]{:S(2)}) collective-permute-start(f32[48,512]{1,0:T(8,128)S(1)} %get-tuple-element.38), channel_id=1, source_target_pairs={{0,1},{1,0},{2,3},{3,2},{4,5},{5,4},{6,7},{7,6},{8,9},{9,8},{10,11... | collective-permute-start | bytes 294920 | tf_op jit(solution)/shard_map/ppermute | solution.py:363
  17.5 0.1 core_sum_first.1.rest_0_.own
  17.6 1.6 %collective-permute-start.8 = (f16[48,1280]{1,0:T(8,128)(2,1)S(1)}, f16[48,1280]{1,0:T(8,128)(2,1)S(1)}, u32[]{:S(2)}, u32[]{:S(2)}) collective-permute-start(f16[48,1280]{1,0:T(8,128)(2,1)S(1)} %convert_element_type.13), channel_id=1, source_target_pairs={{0,2},{1,3},{2,0},{3,1},{4,6},{5,7},{6,4},{7,5},{8,10},{9,11},{10,... | collective-permute-start | bytes 368648 | tf_op jit(solution)/shard_map/ppermute | solution.py:363
  19.2 2.3 %forward_next.3 = (f32[48,384]{1,0:T(8,128)S(1)}, f32[48,384]{1,0:T(8,128)S(1)}, f32[48,512]{1,0:T(8,128)S(1)}, f32[48,512]{1,0:T(8,128)S(1)}) custom-call(bf16[32,1536]{1,0:T(8,128)(2,1)S(1)} %get-tuple-element.35.x.rows_x, bf16[32,1536]{1,0:T(8,128)(2,1)S(1)} %get-tuple-element.36.dy, bf16[2688,1536]{1,0:T(8,128)(2,1)S(1)} %copy-done, ...), custom_call_target="tpu_custom_call" | custom-call | flops 2113929216 | tf_op jit(solution)/shard_map/forward_next/pallas_call | solution.py:401
  21.5 0.0 collective-permute-start.6
  21.5 0.5 %collective-permute-start.5 = (f32[48,384]{1,0:T(8,128)S(1)}, f32[48,384]{1,0:T(8,128)S(1)}, u32[]{:S(2)}, u32[]{:S(2)}) collective-permute-start(f32[48,384]{1,0:T(8,128)S(1)} %get-tuple-element.42), channel_id=1, source_target_pairs={{0,1},{1,0},{2,3},{3,2},{4,5},{5,4},{6,7},{7,6},{8,9},{9,8},{10,11... | collective-permute-start | bytes 221192 | tf_op jit(solution)/shard_map/ppermute | solution.py:363
  22.0 0.9 %collective-permute-done.5.refs_3_ = f32[48,384]{1,0:T(8,128)S(1)} collective-permute-done((f32[48,384]{1,0:T(8,128)S(1)}, f32[48,384]{1,0:T(8,128)S(1)}, u32[]{:S(2)}, u32[]{:S(2)}) %collective-permute-start.5) | collective-permute-done | bytes 73760 | tf_op jit(solution)/shard_map/ppermute | solution.py:363
  22.9 0.1 core_sum_last.1.after.own
  23.0 0.6 %collective-permute-start.7 = (f16[48,1408]{1,0:T(8,128)(2,1)S(1)}, f16[48,1408]{1,0:T(8,128)(2,1)S(1)}, u32[]{:S(2)}, u32[]{:S(2)}) collective-permute-start(f16[48,1408]{1,0:T(8,128)(2,1)S(1)} %convert_element_type.12), channel_id=1, source_target_pairs={{0,2},{1,3},{2,0},{3,1},{4,6},{5,7},{6,4},{7,5},{8,10},{9,11},{10,... | collective-permute-start | bytes 405512 | tf_op jit(solution)/shard_map/ppermute | solution.py:363
  23.7 0.1 activations_first.1
  23.8 0.1 collective-permute-start.9
  24.0 1.3 %collective-permute-done.9.theirs = bf16[48,1280]{1,0:T(8,128)(2,1)S(1)} collective-permute-done((bf16[48,1280]{1,0:T(8,128)(2,1)S(1)}, bf16[48,1280]{1,0:T(8,128)(2,1)S(1)}, u32[]{:S(2)}, u32[]{:S(2)}) %collective-permute-start.9) | collective-permute-done | bytes 122912 | tf_op jit(solution)/shard_map/ppermute | solution.py:363
  25.2 3.7 %gradients_first.1 = (f32[32,1536]{1,0:T(8,128)S(1)}, bf16[2688,1536]{1,0:T(8,128)(2,1)}, bf16[2688,1536]{1,0:T(8,128)(2,1)}) custom-call(bf16[48,1280]{1,0:T(8,128)(2,1)S(1)} %get-tuple-element.46.mine, bf16[48,1280]{1,0:T(8,128)(2,1)S(1)} %collective-permute-done.9.theirs, bf16[32,1536]{1,0:T(8,128)(2,1)S(1)} %get-tuple-element.35.x.rows_x, ...), custom_call_target="tpu_custom_call" | custom-call | tf_op jit(solution)/shard_map/gradients_first/pallas_call | solution.py:451
  29.0 0.2 activations_last.1.after.mine
  29.2 0.2 collective-permute-start.10
  29.4 1.2 %up_gradient_first.1.up_here = bf16[1280,1536]{1,0:T(8,128)(2,1)S(1)} custom-call(bf16[48,1280]{1,0:T(8,128)(2,1)S(1)} %get-tuple-element.46.mine, bf16[48,1280]{1,0:T(8,128)(2,1)S(1)} %collective-permute-done.9.theirs, bf16[32,1536]{1,0:T(8,128)(2,1)S(1)} %get-tuple-element.35.x.rows_x, bf16[48,1536]{1,0:T(8,128)(2,1)S(1)} %activations_last.1.after.mine), custom_call_target="tpu_custom_call" | custom-call | tf_op jit(solution)/shard_map/up_gradient_first/pallas_call | solution.py:401
  30.6 1.9 %gradients_last.1 = (f32[8,1664]{1,0:T(8,128)S(1)}, f32[8,1664]{1,0:T(8,128)S(1)}, f32[8,1664]{1,0:T(8,128)S(1)}, f32[8,1664]{1,0:T(8,128)S(1)}, bf16[2688,1536]{1,0:T(8,128)(2,1)}) custom-call(bf16[48,1536]{1,0:T(8,128)(2,1)S(1)} %activations_last.1.after.mine, bf16[48,1536]{1,0:T(8,128)(2,1)S(1)} %collective-permute-done.10.theirs, ...), custom_call_target="tpu_custom_call" | custom-call | tf_op jit(solution)/shard_map/gradients_last/pallas_call | solution.py:477
  32.6 2.3 %collective-permute-start.11 = (f32[8,1664]{1,0:T(8,128)S(1)}, f32[8,1664]{1,0:T(8,128)S(1)}, u32[]{:S(2)}, u32[]{:S(2)}) collective-permute-start(f32[8,1664]{1,0:T(8,128)S(1)} %get-tuple-element.52), channel_id=1, source_target_pairs={{0,12},{4,8},{8,4},{12,0},{1,13},{5,9},{9,5},{13,1},{2,14},{6,10},... | collective-permute-start | bytes 159752 | tf_op jit(solution)/shard_map/ppermute | solution.py:363
  34.9 2.2 %collective-permute-start.13 = (f32[8,1664]{1,0:T(8,128)S(1)}, f32[8,1664]{1,0:T(8,128)S(1)}, u32[]{:S(2)}, u32[]{:S(2)}) collective-permute-start(f32[8,1664]{1,0:T(8,128)S(1)} %get-tuple-element.54), channel_id=1, source_target_pairs={{0,4},{4,0},{8,12},{12,8},{1,5},{5,1},{9,13},{13,9},{2,6},{6,2},{1... | collective-permute-start | bytes 159752 | tf_op jit(solution)/shard_map/ppermute | solution.py:363
  37.0 3.9 %gradients_rest.1 = (bf16[1408,1536]{1,0:T(8,128)(2,1)S(1)}, bf16[2688,1536]{1,0:T(8,128)(2,1)}, bf16[2688,1536]{1,0:T(8,128)(2,1)}) custom-call(bf16[48,1536]{1,0:T(8,128)(2,1)S(1)} %activations_last.1.after.mine, bf16[48,1536]{1,0:T(8,128)(2,1)S(1)} %collective-permute-done.10.theirs, ...), custom_call_target="tpu_custom_call", output_to_operand_aliasing={{1}: (4, {}), {2}: (5, {})} | custom-call | flops 3321888768 | tf_op jit(solution)/shard_map/gradients_rest/pallas_call | solution.py:488
  41.0 2.2 %place_rows.1 = (bf16[128,1536]{1,0:T(8,128)(2,1)}, f32[4,128]{1,0:T(4,128)}, bf16[2688,1536]{1,0:T(8,128)(2,1)}) custom-call(bf16[128,128]{1,0:T(8,128)(2,1)S(1)} %triangle.1.up_to, s32[4,128]{1,0:T(4,128)S(1)} %bitcast.4, f32[8,1664]{1,0:T(8,128)S(1)} %collective-permute-done.11.r3, ...), custom_call_target="tpu_custom_call", output_to_operand_aliasing={{2}: (7, {})} | custom-call | tf_op jit(solution)/shard_map/place_rows/pallas_call | solution.py:503
  (28 shorter events, 0.2 us)
Async XLA Ops:
  0.6 0.7 %copy-start.5 = (s32[128,4]{0,1:T(4,128)S(1)}, s32[128,4]{0,1:T(4,128)}, u32[]{:S(2)}) copy-start(s32[128,4]{0,1:T(4,128)} %param.9) | copy-start | bytes 6148
  0.6 0.7 %copy-start.6 = (bf16[128,4]{0,1:T(4,128)(2,1)S(1)}, bf16[128,4]{0,1:T(4,128)(2,1)}, u32[]{:S(2)}) copy-start(bf16[128,4]{0,1:T(4,128)(2,1)} %param.10) | copy-start | bytes 3076
  0.7 1.0 %copy-start.3 = (bf16[128,1536]{1,0:T(8,128)(2,1)S(1)}, bf16[128,1536]{1,0:T(8,128)(2,1)}, u32[]{:S(2)}) copy-start(bf16[128,1536]{1,0:T(8,128)(2,1)} %tokens.1) | copy-start | bytes 1179652
  0.7 1.1 %copy-start.4 = (bf16[128,1536]{1,0:T(8,128)(2,1)S(1)}, bf16[128,1536]{1,0:T(8,128)(2,1)}, u32[]{:S(2)}) copy-start(bf16[128,1536]{1,0:T(8,128)(2,1)} %cotangent.1) | copy-start | bytes 1179652
  0.7 11.5 %copy-start = (bf16[2688,1536]{1,0:T(8,128)(2,1)S(1)}, bf16[2688,1536]{1,0:T(8,128)(2,1)}, u32[]{:S(2)}) copy-start(bf16[2688,1536]{1,0:T(8,128)(2,1)} %w_gate.9) | copy-start | bytes 24772612
  0.7 11.5 %copy-start.1 = (bf16[2688,1536]{1,0:T(8,128)(2,1)S(1)}, bf16[2688,1536]{1,0:T(8,128)(2,1)}, u32[]{:S(2)}) copy-start(bf16[2688,1536]{1,0:T(8,128)(2,1)} %w_up.9) | copy-start | bytes 24772612
  0.7 11.5 %copy-start.2 = (bf16[2688,1536]{1,0:T(8,128)(2,1)S(1)}, bf16[2688,1536]{1,0:T(8,128)(2,1)}, u32[]{:S(2)}) copy-start(bf16[2688,1536]{1,0:T(8,128)(2,1)} %w_down.5) | copy-start | bytes 24772612
  2.1 7.4 %collective-permute-start = (bf16[8,3200]{1,0:T(8,128)(2,1)S(1)}, bf16[8,3200]{1,0:T(8,128)(2,1)S(1)}, u32[]{:S(2)}, u32[]{:S(2)}) collective-permute-start(bf16[8,3200]{1,0:T(8,128)(2,1)S(1)} %pick_rows.1.b0), channel_id=1, source_target_pairs={{0,12},{4,8},{8,4},{12,0},{1,13},{5,9},{9,5},{13,1},{2,14},{6,10},... | collective-permute-start | bytes 153608 | tf_op jit(solution)/shard_map/ppermute | solution.py:363
  7.2 5.0 %collective-permute-start.1 = (bf16[8,3200]{1,0:T(8,128)(2,1)S(1)}, bf16[8,3200]{1,0:T(8,128)(2,1)S(1)}, u32[]{:S(2)}, u32[]{:S(2)}) collective-permute-start(bf16[8,3200]{1,0:T(8,128)(2,1)S(1)} %pick_rows.1.b0), channel_id=1, source_target_pairs={{0,8},{4,12},{8,0},{12,4},{1,9},{5,13},{9,1},{13,5},{2,10},{6,14},... | collective-permute-start | bytes 153608 | tf_op jit(solution)/shard_map/ppermute | solution.py:363
  7.2 5.0 %collective-permute-start.2 = (bf16[8,3200]{1,0:T(8,128)(2,1)S(1)}, bf16[8,3200]{1,0:T(8,128)(2,1)S(1)}, u32[]{:S(2)}, u32[]{:S(2)}) collective-permute-start(bf16[8,3200]{1,0:T(8,128)(2,1)S(1)} %pick_rows.1.b0), channel_id=1, source_target_pairs={{0,4},{4,0},{8,12},{12,8},{1,5},{5,1},{9,13},{13,9},{2,6},{6,2},{1... | collective-permute-start | bytes 153608 | tf_op jit(solution)/shard_map/ppermute | solution.py:363
  15.5 2.0 %collective-permute-start.4 = (f32[48,1280]{1,0:T(8,128)S(1)}, f32[48,1280]{1,0:T(8,128)S(1)}, u32[]{:S(2)}, u32[]{:S(2)}) collective-permute-start(f32[48,1280]{1,0:T(8,128)S(1)} %get-tuple-element.40), channel_id=1, source_target_pairs={{0,1},{1,0},{2,3},{3,2},{4,5},{5,4},{6,7},{7,6},{8,9},{9,8},{10,11... | collective-permute-start | bytes 737288 | tf_op jit(solution)/shard_map/ppermute | solution.py:363
  17.0 5.1 %collective-permute-start.3 = (f32[48,512]{1,0:T(8,128)S(1)}, f32[48,512]{1,0:T(8,128)S(1)}, u32[]{:S(2)}, u32[]{:S(2)}) collective-permute-start(f32[48,512]{1,0:T(8,128)S(1)} %get-tuple-element.38), channel_id=1, source_target_pairs={{0,1},{1,0},{2,3},{3,2},{4,5},{5,4},{6,7},{7,6},{8,9},{9,8},{10,11... | collective-permute-start | bytes 294920 | tf_op jit(solution)/shard_map/ppermute | solution.py:363
  17.6 6.0 %collective-permute-start.8 = (f16[48,1280]{1,0:T(8,128)(2,1)S(1)}, f16[48,1280]{1,0:T(8,128)(2,1)S(1)}, u32[]{:S(2)}, u32[]{:S(2)}) collective-permute-start(f16[48,1280]{1,0:T(8,128)(2,1)S(1)} %convert_element_type.13), channel_id=1, source_target_pairs={{0,2},{1,3},{2,0},{3,1},{4,6},{5,7},{6,4},{7,5},{8,10},{9,11},{10,... | collective-permute-start | bytes 368648 | tf_op jit(solution)/shard_map/ppermute | solution.py:363
  21.5 1.5 %collective-permute-start.6 = (f32[48,512]{1,0:T(8,128)S(1)}, f32[48,512]{1,0:T(8,128)S(1)}, u32[]{:S(2)}, u32[]{:S(2)}) collective-permute-start(f32[48,512]{1,0:T(8,128)S(1)} %get-tuple-element.44), channel_id=1, source_target_pairs={{0,1},{1,0},{2,3},{3,2},{4,5},{5,4},{6,7},{7,6},{8,9},{9,8},{10,11... | collective-permute-start | bytes 294920 | tf_op jit(solution)/shard_map/ppermute | solution.py:363
  21.5 1.4 %collective-permute-start.5 = (f32[48,384]{1,0:T(8,128)S(1)}, f32[48,384]{1,0:T(8,128)S(1)}, u32[]{:S(2)}, u32[]{:S(2)}) collective-permute-start(f32[48,384]{1,0:T(8,128)S(1)} %get-tuple-element.42), channel_id=1, source_target_pairs={{0,1},{1,0},{2,3},{3,2},{4,5},{5,4},{6,7},{7,6},{8,9},{9,8},{10,11... | collective-permute-start | bytes 221192 | tf_op jit(solution)/shard_map/ppermute | solution.py:363
  23.0 5.9 %collective-permute-start.7 = (f16[48,1408]{1,0:T(8,128)(2,1)S(1)}, f16[48,1408]{1,0:T(8,128)(2,1)S(1)}, u32[]{:S(2)}, u32[]{:S(2)}) collective-permute-start(f16[48,1408]{1,0:T(8,128)(2,1)S(1)} %convert_element_type.12), channel_id=1, source_target_pairs={{0,2},{1,3},{2,0},{3,1},{4,6},{5,7},{6,4},{7,5},{8,10},{9,11},{10,... | collective-permute-start | bytes 405512 | tf_op jit(solution)/shard_map/ppermute | solution.py:363
  23.8 1.4 %collective-permute-start.9 = (bf16[48,1280]{1,0:T(8,128)(2,1)S(1)}, bf16[48,1280]{1,0:T(8,128)(2,1)S(1)}, u32[]{:S(2)}, u32[]{:S(2)}) collective-permute-start(bf16[48,1280]{1,0:T(8,128)(2,1)S(1)} %get-tuple-element.46.mine), channel_id=1, source_target_pairs={{0,1},{1,0},{2,3},{3,2},{4,5},{5,4},{6,7},{7,6},{8,9},{9,8},{10,11... | collective-permute-start | bytes 368648 | tf_op jit(solution)/shard_map/ppermute | solution.py:363
  29.2 1.4 %collective-permute-start.10 = (bf16[48,1536]{1,0:T(8,128)(2,1)S(1)}, bf16[48,1536]{1,0:T(8,128)(2,1)S(1)}, u32[]{:S(2)}, u32[]{:S(2)}) collective-permute-start(bf16[48,1536]{1,0:T(8,128)(2,1)S(1)} %activations_last.1.after.mine), channel_id=1, source_target_pairs={{0,1},{1,0},{2,3},{3,2},{4,5},{5,4},{6,7},{7,6},{8,9},{9,8},{10,11... | collective-permute-start | bytes 442376 | tf_op jit(solution)/shard_map/ppermute | solution.py:363
  32.6 8.4 %collective-permute-start.11 = (f32[8,1664]{1,0:T(8,128)S(1)}, f32[8,1664]{1,0:T(8,128)S(1)}, u32[]{:S(2)}, u32[]{:S(2)}) collective-permute-start(f32[8,1664]{1,0:T(8,128)S(1)} %get-tuple-element.52), channel_id=1, source_target_pairs={{0,12},{4,8},{8,4},{12,0},{1,13},{5,9},{9,5},{13,1},{2,14},{6,10},... | collective-permute-start | bytes 159752 | tf_op jit(solution)/shard_map/ppermute | solution.py:363
  34.9 6.1 %collective-permute-start.12 = (f32[8,1664]{1,0:T(8,128)S(1)}, f32[8,1664]{1,0:T(8,128)S(1)}, u32[]{:S(2)}, u32[]{:S(2)}) collective-permute-start(f32[8,1664]{1,0:T(8,128)S(1)} %get-tuple-element.53), channel_id=1, source_target_pairs={{0,8},{4,12},{8,0},{12,4},{1,9},{5,13},{9,1},{13,5},{2,10},{6,14},... | collective-permute-start | bytes 159752 | tf_op jit(solution)/shard_map/ppermute | solution.py:363
  34.9 6.1 %collective-permute-start.13 = (f32[8,1664]{1,0:T(8,128)S(1)}, f32[8,1664]{1,0:T(8,128)S(1)}, u32[]{:S(2)}, u32[]{:S(2)}) collective-permute-start(f32[8,1664]{1,0:T(8,128)S(1)} %get-tuple-element.54), channel_id=1, source_target_pairs={{0,4},{4,0},{8,12},{12,8},{1,5},{5,1},{9,13},{13,9},{2,6},{6,2},{1... | collective-permute-start | bytes 159752 | tf_op jit(solution)/shard_map/ppermute | solution.py:363

commit v2 on v1

--- a/solution.py
+++ b/solution.py
@@ -106,8 +106,12 @@
     up_to[...] = jnp.where(here, F32(1.0), F32(0.0)).astype(BF16)
 
 
-def pick_kernel(up_to, routes, probs, tokens, cotangent, sent):
-    chosen, hits = slots_of(routes[...], up_to[...])
+def slots_kernel(up_to, routes, hits):
+    hits[...] = slots_of(routes[...], up_to[...])[1]
+
+
+def pick_kernel(hits_in, routes, probs, tokens, cotangent, sent):
+    chosen, hits = routes[...] == 0, hits_in[...]
     weight = jnp.sum(jnp.where(chosen, probs[...].astype(F32), F32(0.0)), axis=0, keepdims=True)
     picker = hits.astype(BF16)
     width = tokens.shape[1]
@@ -316,7 +320,7 @@
 
 
 def place_kernel(
-    cut, up_to, routes, r3, r2, r1, r0, up_here, up_before,
+    cut, hits, routes, r2, r3, r1, r0, up_here, up_before,
     grad_tokens, grad_probs, grad_up, placed, placed_probs, sems,
 ):
     core = lax.rem(lax.axis_index("hidden"), 2)
@@ -330,11 +334,11 @@
 
     @pl.when(core < 2)
     def place():
-        chosen, hits = slots_of(routes[...], up_to[...])
+        chosen = routes[...] == 0
         total = r0[...] + r1[...] + r2[...] + r3[...]
         width = grad_tokens.shape[1]
-        placed[...] = contract_first(hits.astype(BF16), total[:, :width].astype(BF16)).astype(BF16)
-        token_dots = jnp.sum(hits * total[:, width : width + 1], axis=0, keepdims=True)
+        placed[...] = contract_first(hits[...].astype(BF16), total[:, :width].astype(BF16)).astype(BF16)
+        token_dots = jnp.sum(hits[...] * total[:, width : width + 1], axis=0, keepdims=True)
         placed_probs[...] = jnp.where(chosen, token_dots, F32(0.0))
 
     for copy in copies:
@@ -371,6 +375,14 @@
         cost_estimate=pl.CostEstimate(flops=WAIT_FLOPS, bytes_accessed=0, transcendentals=0),
         name="triangle",
     )()
+    hits = pl.pallas_call(
+        slots_kernel,
+        in_specs=[VMEM] * 2,
+        out_specs=VMEM,
+        out_shape=shape((CAP, tokens_here), F32),
+        compiler_params=params(1),
+        name="find_slots",
+    )(up_to, routes_t)
     sent = pl.pallas_call(
         pick_kernel,
         in_specs=[VMEM] * 5,
@@ -378,7 +390,7 @@
         out_shape=shape((CAP, 2 * width + LANES), BF16),
         compiler_params=params(2),
         name="pick_rows",
-    )(up_to, routes_t, probs_t, tokens, cotangent)
+    )(hits, routes_t, probs_t, tokens, cotangent)
     got = [swap(sent, "expert", bit) for bit in (3, 2, 1)]
 
     def exchange(own):
@@ -483,7 +495,7 @@
         compiler_params=params(4),
         name="gradients_last",
     )(*last, w_gate, w_up, term, up_first)
-    back = [swap(parts[bit], "expert", bit) for bit in (3, 2, 1)]
+    back = [swap(parts[bit], "expert", bit) for bit in (2, 3, 1)]
 
     up_last, grad_down, grad_gate = pl.pallas_call(
         functools.partial(gradients_rest_kernel, cut),
@@ -513,7 +525,7 @@
         input_output_aliases={7: 2},
         compiler_params=params(4),
         name="place_rows",
-    )(up_to, routes_t, *back, parts[0], up_last, up_a)
+    )(hits, routes_t, *back, parts[0], up_last, up_a)
     return (grad_tokens, grad_probs.T, grad_gate, grad_up, grad_down)
 
 

time: 43.4 us -> 43.3 us (level)
  waiting for transfers between devices: 6.63 us -> 7.56 us
  starting transfers between devices: 13.8 us -> 12.9 us
    ppermute x14, waiting for transfers between devices: 6.63 us -> 7.56 us  [swap(): return lax.ppermute(value, axis, [(i, i ^ bit) for i in range(4)])]
    ppermute x14, starting transfers between devices: 13.8 us -> 12.9 us  [swap(): return lax.ppermute(value, axis, [(i, i ^ bit) for i in range(4)])]
  transfers between devices with their start and end apart: 14 -> 14, of which waited for: 4 -> 6; matrix products, arithmetic and copies ran while one was open for 0% -> 0% of each run, Pallas kernels for 30% -> 30%
where the time goes in v2:
time: 43.3 us; the launch traced here: 43.1 us
  Pallas kernels  20.8 us (48%)
  starting transfers between devices  12.9 us (30%)
  waiting for transfers between devices  7.56 us (17%)
  local copies, waits for them, and re-layouts  0.95 us (2%)
  between operations  0.81 us (2%)
    ppermute x14, starting transfers between devices, swap(): return lax.ppermute(value, axis, [(i, i ^ bit) for i in range(4)])  12.9 us
    pallas_call x8, Pallas kernels, call(): pl.pallas_call(kernel, in_specs=[VMEM] * len(args), out_specs=VMEM if sin...  8.71 us
    ppermute x14, waiting for transfers between devices, swap(): return lax.ppermute(value, axis, [(i, i ^ bit) for i in range(4)])  7.56 us
    pallas_call x1, Pallas kernels, paired_shards(): pl.pallas_call(functools.partial(gradients_rest_kernel, cut), in_specs=[V...  3.93 us
    pallas_call x1, Pallas kernels, paired_shards(): pl.pallas_call(functools.partial(gradients_first_kernel, cut), in_specs=[...  3.7 us
    pallas_call x1, Pallas kernels, paired_shards(): pl.pallas_call(functools.partial(place_kernel, cut), in_specs=[VMEM] * 7...  2.2 us
    pallas_call x1, Pallas kernels, paired_shards(): pl.pallas_call(functools.partial(gradients_last_kernel, cut), in_specs=[V...  1.93 us
    unnamed x14, local copies, waits for them, and re-layouts  0.95 us
  transfers between devices with their start and end apart: 14, of which 6 were waited for; matrix products, arithmetic and copies ran while one was open for 0% of the time, Pallas kernels for 30%

profile of v2, /device:TPU:0, one launch (start us, length us, event | category | flops | bytes accessed | tf_op | source)
XLA Modules:
  0.0 43.1 jit_solution(470917872395304007)
XLA Ops:
  0.7 0.6 %copy-done.5 = s32[128,4]{0,1:T(4,128)S(1)} copy-done((s32[128,4]{0,1:T(4,128)S(1)}, s32[128,4]{0,1:T(4,128)}, u32[]{:S(2)}) %copy-start.5) | copy-done | bytes 2072
  1.3 0.1 find_slots.1.hits_in.hits
  1.4 0.2 copy-done.3
  1.7 0.1 copy-done.4
  1.8 0.2 pick_rows.1.b0
  2.0 5.1 %collective-permute-start = (bf16[8,3200]{1,0:T(8,128)(2,1)S(1)}, bf16[8,3200]{1,0:T(8,128)(2,1)S(1)}, u32[]{:S(2)}, u32[]{:S(2)}) collective-permute-start(bf16[8,3200]{1,0:T(8,128)(2,1)S(1)} %pick_rows.1.b0), channel_id=1, source_target_pairs={{0,12},{4,8},{8,4},{12,0},{1,13},{5,9},{9,5},{13,1},{2,14},{6,10},... | collective-permute-start | bytes 153608 | tf_op jit(solution)/shard_map/ppermute | solution.py:367
  7.1 0.6 %collective-permute-start.2 = (bf16[8,3200]{1,0:T(8,128)(2,1)S(1)}, bf16[8,3200]{1,0:T(8,128)(2,1)S(1)}, u32[]{:S(2)}, u32[]{:S(2)}) collective-permute-start(bf16[8,3200]{1,0:T(8,128)(2,1)S(1)} %pick_rows.1.b0), channel_id=1, source_target_pairs={{0,4},{4,0},{8,12},{12,8},{1,5},{5,1},{9,13},{13,9},{2,6},{6,2},{1... | collective-permute-start | bytes 153608 | tf_op jit(solution)/shard_map/ppermute | solution.py:367
  7.7 1.6 %collective-permute-done.b3 = bf16[8,3200]{1,0:T(8,128)(2,1)S(1)} collective-permute-done((bf16[8,3200]{1,0:T(8,128)(2,1)S(1)}, bf16[8,3200]{1,0:T(8,128)(2,1)S(1)}, u32[]{:S(2)}, u32[]{:S(2)}) %collective-permute-start) | collective-permute-done | bytes 51232 | tf_op jit(solution)/shard_map/ppermute | solution.py:367
  9.3 2.7 %collective-permute-done.1.b2 = bf16[8,3200]{1,0:T(8,128)(2,1)S(1)} collective-permute-done((bf16[8,3200]{1,0:T(8,128)(2,1)S(1)}, bf16[8,3200]{1,0:T(8,128)(2,1)S(1)}, u32[]{:S(2)}, u32[]{:S(2)}) %collective-permute-start.1) | collective-permute-done | bytes 51232 | tf_op jit(solution)/shard_map/ppermute | solution.py:367
  12.1 3.3 %forward_first.1 = (bf16[32,1536]{1,0:T(8,128)(2,1)S(1)}, bf16[32,1536]{1,0:T(8,128)(2,1)S(1)}, bf16[32,1536]{1,0:T(8,128)(2,1)S(1)}, f32[32,128]{1,0:T(8,128)S(...) custom-call(bf16[8,3200]{1,0:T(8,128)(2,1)S(1)} %collective-permute-done.b3, ...), custom_call_target="tpu_custom_call" | custom-call | flops 3019898880 | tf_op jit(solution)/shard_map/forward_first/pallas_call | solution.py:413
  15.4 1.4 %forward_next.2 = (f32[48,512]{1,0:T(8,128)S(1)}, f32[48,512]{1,0:T(8,128)S(1)}) custom-call(bf16[32,1536]{1,0:T(8,128)(2,1)S(1)} %get-tuple-element.35.x.rows_x, bf16[32,1536]{1,0:T(8,128)(2,1)S(1)} %get-tuple-element.36.dy, bf16[2688,1536]{1,0:T(8,128)(2,1)S(1)} %copy-done, bf16[2688,1536]{1,0:T(8,128)(2,1)S(1)} %copy-done.1, bf16[2688,1536]{1,0:T(8,128)(2,1)S(1)} %copy-done.2), custom_call_target="tpu_custom_call" | custom-call | flops 1207959552 | tf_op jit(solution)/shard_map/forward_next/pallas_call | solution.py:413
  16.9 0.5 %collective-permute-start.3 = (f32[48,512]{1,0:T(8,128)S(1)}, f32[48,512]{1,0:T(8,128)S(1)}, u32[]{:S(2)}, u32[]{:S(2)}) collective-permute-start(f32[48,512]{1,0:T(8,128)S(1)} %get-tuple-element.38), channel_id=1, source_target_pairs={{0,1},{1,0},{2,3},{3,2},{4,5},{5,4},{6,7},{7,6},{8,9},{9,8},{10,11... | collective-permute-start | bytes 294920 | tf_op jit(solution)/shard_map/ppermute | solution.py:367
  17.5 1.5 %collective-permute-start.8 = (f16[48,1280]{1,0:T(8,128)(2,1)S(1)}, f16[48,1280]{1,0:T(8,128)(2,1)S(1)}, u32[]{:S(2)}, u32[]{:S(2)}) collective-permute-start(f16[48,1280]{1,0:T(8,128)(2,1)S(1)} %convert_element_type.13), channel_id=1, source_target_pairs={{0,2},{1,3},{2,0},{3,1},{4,6},{5,7},{6,4},{7,5},{8,10},{9,11},{10,... | collective-permute-start | bytes 368648 | tf_op jit(solution)/shard_map/ppermute | solution.py:367
  19.0 2.3 %forward_next.3 = (f32[48,384]{1,0:T(8,128)S(1)}, f32[48,384]{1,0:T(8,128)S(1)}, f32[48,512]{1,0:T(8,128)S(1)}, f32[48,512]{1,0:T(8,128)S(1)}) custom-call(bf16[32,1536]{1,0:T(8,128)(2,1)S(1)} %get-tuple-element.35.x.rows_x, bf16[32,1536]{1,0:T(8,128)(2,1)S(1)} %get-tuple-element.36.dy, bf16[2688,1536]{1,0:T(8,128)(2,1)S(1)} %copy-done, ...), custom_call_target="tpu_custom_call" | custom-call | flops 2113929216 | tf_op jit(solution)/shard_map/forward_next/pallas_call | solution.py:413
  21.4 0.5 %collective-permute-start.5 = (f32[48,384]{1,0:T(8,128)S(1)}, f32[48,384]{1,0:T(8,128)S(1)}, u32[]{:S(2)}, u32[]{:S(2)}) collective-permute-start(f32[48,384]{1,0:T(8,128)S(1)} %get-tuple-element.42), channel_id=1, source_target_pairs={{0,1},{1,0},{2,3},{3,2},{4,5},{5,4},{6,7},{7,6},{8,9},{9,8},{10,11... | collective-permute-start | bytes 221192 | tf_op jit(solution)/shard_map/ppermute | solution.py:367
  21.9 0.9 %collective-permute-done.5.refs_3_ = f32[48,384]{1,0:T(8,128)S(1)} collective-permute-done((f32[48,384]{1,0:T(8,128)S(1)}, f32[48,384]{1,0:T(8,128)S(1)}, u32[]{:S(2)}, u32[]{:S(2)}) %collective-permute-start.5) | collective-permute-done | bytes 73760 | tf_op jit(solution)/shard_map/ppermute | solution.py:367
  22.9 0.6 %collective-permute-start.7 = (f16[48,1408]{1,0:T(8,128)(2,1)S(1)}, f16[48,1408]{1,0:T(8,128)(2,1)S(1)}, u32[]{:S(2)}, u32[]{:S(2)}) collective-permute-start(f16[48,1408]{1,0:T(8,128)(2,1)S(1)} %convert_element_type.12), channel_id=1, source_target_pairs={{0,2},{1,3},{2,0},{3,1},{4,6},{5,7},{6,4},{7,5},{8,10},{9,11},{10,... | collective-permute-start | bytes 405512 | tf_op jit(solution)/shard_map/ppermute | solution.py:367
  23.6 0.1 activations_first.1
  23.7 0.1 collective-permute-start.9
  23.8 1.3 %collective-permute-done.9.theirs = bf16[48,1280]{1,0:T(8,128)(2,1)S(1)} collective-permute-done((bf16[48,1280]{1,0:T(8,128)(2,1)S(1)}, bf16[48,1280]{1,0:T(8,128)(2,1)S(1)}, u32[]{:S(2)}, u32[]{:S(2)}) %collective-permute-start.9) | collective-permute-done | bytes 122912 | tf_op jit(solution)/shard_map/ppermute | solution.py:367
  25.1 3.7 %gradients_first.1 = (f32[32,1536]{1,0:T(8,128)S(1)}, bf16[2688,1536]{1,0:T(8,128)(2,1)}, bf16[2688,1536]{1,0:T(8,128)(2,1)}) custom-call(bf16[48,1280]{1,0:T(8,128)(2,1)S(1)} %get-tuple-element.46.mine, bf16[48,1280]{1,0:T(8,128)(2,1)S(1)} %collective-permute-done.9.theirs, bf16[32,1536]{1,0:T(8,128)(2,1)S(1)} %get-tuple-element.35.x.rows_x, ...), custom_call_target="tpu_custom_call" | custom-call | tf_op jit(solution)/shard_map/gradients_first/pallas_call | solution.py:463
  28.9 0.2 activations_last.1.after.mine
  29.1 0.2 collective-permute-start.10
  29.3 1.2 %up_gradient_first.1.up_here = bf16[1280,1536]{1,0:T(8,128)(2,1)S(1)} custom-call(bf16[48,1280]{1,0:T(8,128)(2,1)S(1)} %get-tuple-element.46.mine, bf16[48,1280]{1,0:T(8,128)(2,1)S(1)} %collective-permute-done.9.theirs, bf16[32,1536]{1,0:T(8,128)(2,1)S(1)} %get-tuple-element.35.x.rows_x, bf16[48,1536]{1,0:T(8,128)(2,1)S(1)} %activations_last.1.after.mine), custom_call_target="tpu_custom_call" | custom-call | tf_op jit(solution)/shard_map/up_gradient_first/pallas_call | solution.py:413
  30.5 1.9 %gradients_last.1 = (f32[8,1664]{1,0:T(8,128)S(1)}, f32[8,1664]{1,0:T(8,128)S(1)}, f32[8,1664]{1,0:T(8,128)S(1)}, f32[8,1664]{1,0:T(8,128)S(1)}, bf16[2688,1536]{1,0:T(8,128)(2,1)}) custom-call(bf16[48,1536]{1,0:T(8,128)(2,1)S(1)} %activations_last.1.after.mine, bf16[48,1536]{1,0:T(8,128)(2,1)S(1)} %collective-permute-done.10.theirs, ...), custom_call_target="tpu_custom_call" | custom-call | tf_op jit(solution)/shard_map/gradients_last/pallas_call | solution.py:489
  32.4 2.1 %collective-permute-start.11 = (f32[8,1664]{1,0:T(8,128)S(1)}, f32[8,1664]{1,0:T(8,128)S(1)}, u32[]{:S(2)}, u32[]{:S(2)}) collective-permute-start(f32[8,1664]{1,0:T(8,128)S(1)} %get-tuple-element.52), channel_id=1, source_target_pairs={{0,8},{4,12},{8,0},{12,4},{1,9},{5,13},{9,1},{13,5},{2,10},{6,14},... | collective-permute-start | bytes 159752 | tf_op jit(solution)/shard_map/ppermute | solution.py:367
  34.5 1.1 %collective-permute-start.12 = (f32[8,1664]{1,0:T(8,128)S(1)}, f32[8,1664]{1,0:T(8,128)S(1)}, u32[]{:S(2)}, u32[]{:S(2)}) collective-permute-start(f32[8,1664]{1,0:T(8,128)S(1)} %get-tuple-element.53), channel_id=1, source_target_pairs={{0,12},{4,8},{8,4},{12,0},{1,13},{5,9},{9,5},{13,1},{2,14},{6,10},... | collective-permute-start | bytes 159752 | tf_op jit(solution)/shard_map/ppermute | solution.py:367
  35.6 0.4 collective-permute-start.13
  36.0 3.9 %gradients_rest.1 = (bf16[1408,1536]{1,0:T(8,128)(2,1)S(1)}, bf16[2688,1536]{1,0:T(8,128)(2,1)}, bf16[2688,1536]{1,0:T(8,128)(2,1)}) custom-call(bf16[48,1536]{1,0:T(8,128)(2,1)S(1)} %activations_last.1.after.mine, bf16[48,1536]{1,0:T(8,128)(2,1)S(1)} %collective-permute-done.10.theirs, ...), custom_call_target="tpu_custom_call", output_to_operand_aliasing={{1}: (4, {}), {2}: (5, {})} | custom-call | flops 3321888768 | tf_op jit(solution)/shard_map/gradients_rest/pallas_call | solution.py:500
  40.0 0.8 %collective-permute-done.12.r3 = f32[8,1664]{1,0:T(8,128)S(1)} collective-permute-done((f32[8,1664]{1,0:T(8,128)S(1)}, f32[8,1664]{1,0:T(8,128)S(1)}, u32[]{:S(2)}, u32[]{:S(2)}) %collective-permute-start.12) | collective-permute-done | bytes 53280 | tf_op jit(solution)/shard_map/ppermute | solution.py:367
  40.8 0.2 collective-permute-done.13.r1
  40.9 2.2 %place_rows.1 = (bf16[128,1536]{1,0:T(8,128)(2,1)}, f32[4,128]{1,0:T(4,128)}, bf16[2688,1536]{1,0:T(8,128)(2,1)}) custom-call(f32[8,128]{1,0:T(8,128)S(1)} %find_slots.1.hits_in.hits, s32[4,128]{1,0:T(4,128)S(1)} %bitcast.5, f32[8,1664]{1,0:T(8,128)S(1)} %collective-permute-done.11.r2, ...), custom_call_target="tpu_custom_call", output_to_operand_aliasing={{2}: (7, {})} | custom-call | tf_op jit(solution)/shard_map/place_rows/pallas_call | solution.py:515
  (29 shorter events, 0.4 us)
Async XLA Ops:
  0.6 0.7 %copy-start.5 = (s32[128,4]{0,1:T(4,128)S(1)}, s32[128,4]{0,1:T(4,128)}, u32[]{:S(2)}) copy-start(s32[128,4]{0,1:T(4,128)} %param.9) | copy-start | bytes 6148
  0.6 0.8 %copy-start.6 = (bf16[128,4]{0,1:T(4,128)(2,1)S(1)}, bf16[128,4]{0,1:T(4,128)(2,1)}, u32[]{:S(2)}) copy-start(bf16[128,4]{0,1:T(4,128)(2,1)} %param.10) | copy-start | bytes 3076
  0.7 1.0 %copy-start.3 = (bf16[128,1536]{1,0:T(8,128)(2,1)S(1)}, bf16[128,1536]{1,0:T(8,128)(2,1)}, u32[]{:S(2)}) copy-start(bf16[128,1536]{1,0:T(8,128)(2,1)} %tokens.1) | copy-start | bytes 1179652
  0.7 1.1 %copy-start.4 = (bf16[128,1536]{1,0:T(8,128)(2,1)S(1)}, bf16[128,1536]{1,0:T(8,128)(2,1)}, u32[]{:S(2)}) copy-start(bf16[128,1536]{1,0:T(8,128)(2,1)} %cotangent.1) | copy-start | bytes 1179652
  0.7 11.4 %copy-start = (bf16[2688,1536]{1,0:T(8,128)(2,1)S(1)}, bf16[2688,1536]{1,0:T(8,128)(2,1)}, u32[]{:S(2)}) copy-start(bf16[2688,1536]{1,0:T(8,128)(2,1)} %w_gate.9) | copy-start | bytes 24772612
  0.7 11.4 %copy-start.1 = (bf16[2688,1536]{1,0:T(8,128)(2,1)S(1)}, bf16[2688,1536]{1,0:T(8,128)(2,1)}, u32[]{:S(2)}) copy-start(bf16[2688,1536]{1,0:T(8,128)(2,1)} %w_up.9) | copy-start | bytes 24772612
  0.7 11.4 %copy-start.2 = (bf16[2688,1536]{1,0:T(8,128)(2,1)S(1)}, bf16[2688,1536]{1,0:T(8,128)(2,1)}, u32[]{:S(2)}) copy-start(bf16[2688,1536]{1,0:T(8,128)(2,1)} %w_down.5) | copy-start | bytes 24772612
  2.0 7.4 %collective-permute-start = (bf16[8,3200]{1,0:T(8,128)(2,1)S(1)}, bf16[8,3200]{1,0:T(8,128)(2,1)S(1)}, u32[]{:S(2)}, u32[]{:S(2)}) collective-permute-start(bf16[8,3200]{1,0:T(8,128)(2,1)S(1)} %pick_rows.1.b0), channel_id=1, source_target_pairs={{0,12},{4,8},{8,4},{12,0},{1,13},{5,9},{9,5},{13,1},{2,14},{6,10},... | collective-permute-start | bytes 153608 | tf_op jit(solution)/shard_map/ppermute | solution.py:367
  7.1 5.0 %collective-permute-start.1 = (bf16[8,3200]{1,0:T(8,128)(2,1)S(1)}, bf16[8,3200]{1,0:T(8,128)(2,1)S(1)}, u32[]{:S(2)}, u32[]{:S(2)}) collective-permute-start(bf16[8,3200]{1,0:T(8,128)(2,1)S(1)} %pick_rows.1.b0), channel_id=1, source_target_pairs={{0,8},{4,12},{8,0},{12,4},{1,9},{5,13},{9,1},{13,5},{2,10},{6,14},... | collective-permute-start | bytes 153608 | tf_op jit(solution)/shard_map/ppermute | solution.py:367
  7.1 5.0 %collective-permute-start.2 = (bf16[8,3200]{1,0:T(8,128)(2,1)S(1)}, bf16[8,3200]{1,0:T(8,128)(2,1)S(1)}, u32[]{:S(2)}, u32[]{:S(2)}) collective-permute-start(bf16[8,3200]{1,0:T(8,128)(2,1)S(1)} %pick_rows.1.b0), channel_id=1, source_target_pairs={{0,4},{4,0},{8,12},{12,8},{1,5},{5,1},{9,13},{13,9},{2,6},{6,2},{1... | collective-permute-start | bytes 153608 | tf_op jit(solution)/shard_map/ppermute | solution.py:367
  15.4 2.0 %collective-permute-start.4 = (f32[48,1280]{1,0:T(8,128)S(1)}, f32[48,1280]{1,0:T(8,128)S(1)}, u32[]{:S(2)}, u32[]{:S(2)}) collective-permute-start(f32[48,1280]{1,0:T(8,128)S(1)} %get-tuple-element.40), channel_id=1, source_target_pairs={{0,1},{1,0},{2,3},{3,2},{4,5},{5,4},{6,7},{7,6},{8,9},{9,8},{10,11... | collective-permute-start | bytes 737288 | tf_op jit(solution)/shard_map/ppermute | solution.py:367
  16.9 5.0 %collective-permute-start.3 = (f32[48,512]{1,0:T(8,128)S(1)}, f32[48,512]{1,0:T(8,128)S(1)}, u32[]{:S(2)}, u32[]{:S(2)}) collective-permute-start(f32[48,512]{1,0:T(8,128)S(1)} %get-tuple-element.38), channel_id=1, source_target_pairs={{0,1},{1,0},{2,3},{3,2},{4,5},{5,4},{6,7},{7,6},{8,9},{9,8},{10,11... | collective-permute-start | bytes 294920 | tf_op jit(solution)/shard_map/ppermute | solution.py:367
  17.5 6.0 %collective-permute-start.8 = (f16[48,1280]{1,0:T(8,128)(2,1)S(1)}, f16[48,1280]{1,0:T(8,128)(2,1)S(1)}, u32[]{:S(2)}, u32[]{:S(2)}) collective-permute-start(f16[48,1280]{1,0:T(8,128)(2,1)S(1)} %convert_element_type.13), channel_id=1, source_target_pairs={{0,2},{1,3},{2,0},{3,1},{4,6},{5,7},{6,4},{7,5},{8,10},{9,11},{10,... | collective-permute-start | bytes 368648 | tf_op jit(solution)/shard_map/ppermute | solution.py:367
  21.3 1.5 %collective-permute-start.6 = (f32[48,512]{1,0:T(8,128)S(1)}, f32[48,512]{1,0:T(8,128)S(1)}, u32[]{:S(2)}, u32[]{:S(2)}) collective-permute-start(f32[48,512]{1,0:T(8,128)S(1)} %get-tuple-element.44), channel_id=1, source_target_pairs={{0,1},{1,0},{2,3},{3,2},{4,5},{5,4},{6,7},{7,6},{8,9},{9,8},{10,11... | collective-permute-start | bytes 294920 | tf_op jit(solution)/shard_map/ppermute | solution.py:367
  21.4 1.4 %collective-permute-start.5 = (f32[48,384]{1,0:T(8,128)S(1)}, f32[48,384]{1,0:T(8,128)S(1)}, u32[]{:S(2)}, u32[]{:S(2)}) collective-permute-start(f32[48,384]{1,0:T(8,128)S(1)} %get-tuple-element.42), channel_id=1, source_target_pairs={{0,1},{1,0},{2,3},{3,2},{4,5},{5,4},{6,7},{7,6},{8,9},{9,8},{10,11... | collective-permute-start | bytes 221192 | tf_op jit(solution)/shard_map/ppermute | solution.py:367
  22.9 5.9 %collective-permute-start.7 = (f16[48,1408]{1,0:T(8,128)(2,1)S(1)}, f16[48,1408]{1,0:T(8,128)(2,1)S(1)}, u32[]{:S(2)}, u32[]{:S(2)}) collective-permute-start(f16[48,1408]{1,0:T(8,128)(2,1)S(1)} %convert_element_type.12), channel_id=1, source_target_pairs={{0,2},{1,3},{2,0},{3,1},{4,6},{5,7},{6,4},{7,5},{8,10},{9,11},{10,... | collective-permute-start | bytes 405512 | tf_op jit(solution)/shard_map/ppermute | solution.py:367
  23.7 1.4 %collective-permute-start.9 = (bf16[48,1280]{1,0:T(8,128)(2,1)S(1)}, bf16[48,1280]{1,0:T(8,128)(2,1)S(1)}, u32[]{:S(2)}, u32[]{:S(2)}) collective-permute-start(bf16[48,1280]{1,0:T(8,128)(2,1)S(1)} %get-tuple-element.46.mine), channel_id=1, source_target_pairs={{0,1},{1,0},{2,3},{3,2},{4,5},{5,4},{6,7},{7,6},{8,9},{9,8},{10,11... | collective-permute-start | bytes 368648 | tf_op jit(solution)/shard_map/ppermute | solution.py:367
  29.1 1.4 %collective-permute-start.10 = (bf16[48,1536]{1,0:T(8,128)(2,1)S(1)}, bf16[48,1536]{1,0:T(8,128)(2,1)S(1)}, u32[]{:S(2)}, u32[]{:S(2)}) collective-permute-start(bf16[48,1536]{1,0:T(8,128)(2,1)S(1)} %activations_last.1.after.mine), channel_id=1, source_target_pairs={{0,1},{1,0},{2,3},{3,2},{4,5},{5,4},{6,7},{7,6},{8,9},{9,8},{10,11... | collective-permute-start | bytes 442376 | tf_op jit(solution)/shard_map/ppermute | solution.py:367
  32.4 7.5 %collective-permute-start.11 = (f32[8,1664]{1,0:T(8,128)S(1)}, f32[8,1664]{1,0:T(8,128)S(1)}, u32[]{:S(2)}, u32[]{:S(2)}) collective-permute-start(f32[8,1664]{1,0:T(8,128)S(1)} %get-tuple-element.52), channel_id=1, source_target_pairs={{0,8},{4,12},{8,0},{12,4},{1,9},{5,13},{9,1},{13,5},{2,10},{6,14},... | collective-permute-start | bytes 159752 | tf_op jit(solution)/shard_map/ppermute | solution.py:367
  34.5 6.2 %collective-permute-start.12 = (f32[8,1664]{1,0:T(8,128)S(1)}, f32[8,1664]{1,0:T(8,128)S(1)}, u32[]{:S(2)}, u32[]{:S(2)}) collective-permute-start(f32[8,1664]{1,0:T(8,128)S(1)} %get-tuple-element.53), channel_id=1, source_target_pairs={{0,12},{4,8},{8,4},{12,0},{1,13},{5,9},{9,5},{13,1},{2,14},{6,10},... | collective-permute-start | bytes 159752 | tf_op jit(solution)/shard_map/ppermute | solution.py:367
  35.6 5.3 %collective-permute-start.13 = (f32[8,1664]{1,0:T(8,128)S(1)}, f32[8,1664]{1,0:T(8,128)S(1)}, u32[]{:S(2)}, u32[]{:S(2)}) collective-permute-start(f32[8,1664]{1,0:T(8,128)S(1)} %get-tuple-element.54), channel_id=1, source_target_pairs={{0,4},{4,0},{8,12},{12,8},{1,5},{5,1},{9,13},{13,9},{2,6},{6,2},{1... | collective-permute-start | bytes 159752 | tf_op jit(solution)/shard_map/ppermute | solution.py:367
